TPU v7x, 128 devices: a whole 4x4x4 slice. The times are simulated.
128 devices in a mesh: dp: 64 (over z, y_hi, x, core), expert: 2 (over y_lo).
Axes of the slice: x: 4, y: 4 (y_hi: 2, y_lo: 2; y = y_hi * 2 + y_lo), z: 4, core: 2. Of those that a mesh axis runs over, the one named last changes fastest.
Arguments:
- tokens: bfloat16 [256, 64, 1536], P(('dp', 'expert')), may hold values from -6 to 6
- segment_ids: int32 [256, 64], P(('dp', 'expert')), may hold values from 0 to 7, never falling along the last dimension, each value on 1 to 16 neighbouring positions
- routes: int32 [256, 64, 8], P(('dp', 'expert')), may hold values from 0 to 15, all different within a row
- cotangent: bfloat16 [256, 64, 1536], P(('dp', 'expert')), may hold values from -6 to 6
- attn_gain: bfloat16 [1536], P(('dp', 'expert')), may hold values from 0.5 to 1.5
- query_weight: bfloat16 [1536, 1536], P(('dp', 'expert')), may hold values from -0.15625 to 0.15625
- key_weight: bfloat16 [1536, 512], P(('dp', 'expert')), may hold values from -0.15625 to 0.15625
- value_weight: bfloat16 [1536, 512], P(('dp', 'expert')), may hold values from -0.15625 to 0.15625
- output_weight: bfloat16 [1536, 1536], P(('dp', 'expert')), may hold values from -0.625 to 0.625
- expert_gain: bfloat16 [1536], P(('dp', 'expert')), may hold values from 0.5 to 1.5
- router_weight: bfloat16 [1536, 16], P(('dp', 'expert')), may hold values from -0.078125 to 0.078125
- expert_in: bfloat16 [16, 1536, 1024], P('expert', 'dp'), may hold values from -0.15625 to 0.15625
- expert_out: bfloat16 [16, 512, 1536], P('expert', 'dp'), may hold values from -1 to 1
Outputs:
- block_out: bfloat16 [256, 64, 1536], P(('dp', 'expert'))
- token_grad: bfloat16 [256, 64, 1536], P(('dp', 'expert'))
- attn_gain_grad: float32 [1536], P(('dp', 'expert'))
- query_weight_grad: float32 [1536, 1536], P(('dp', 'expert'))
- key_weight_grad: float32 [1536, 512], P(('dp', 'expert'))
- value_weight_grad: float32 [1536, 512], P(('dp', 'expert'))
- output_weight_grad: float32 [1536, 1536], P(('dp', 'expert'))
- expert_gain_grad: float32 [1536], P(('dp', 'expert'))
- router_weight_grad: float32 [1536, 16], P(('dp', 'expert'))
- expert_in_grad: float32 [16, 1536, 1024], P('expert', 'dp')
- expert_out_grad: float32 [16, 512, 1536], P('expert', 'dp')
Inputs may be any that keep to these rules, and one draw needn't show every extreme that they name: `segment_ids`: positions of segment 0 (padding) come first in a row, then documents 1, 2, ... in order; each segment spans 1 to 16 positions. `routes`: each token names 8 different experts; every expert is named by some token.
All inputs are finite; a program needn't handle non-finite values.
Results may differ from a plain program's by a relative error of at most 0.015.
Values may be sent and summed in bfloat16 or wider, within the bound.
No kernel may reach another device: no remote copies, remote signals or barrier semaphores. Data moves between devices by JAX's collectives and lax.ppermute only.
A program may use at most 320 MiB of HBM per device.

v0:
```python
import jax
import jax.numpy as jnp
from jax import lax
from jax.sharding import PartitionSpec as P

D = 1536
Q_HEADS = 24
KV_HEADS = 8
HEAD_DIM = 64
F = 512
TOPK = 8


norm_eps = 1e-05


def rms_forward(values, gain_vec):
    scale_row = lax.rsqrt(jnp.mean(values * values, axis=-1, keepdims=True) + norm_eps)
    return values * scale_row * gain_vec


def rotary_tables(seq_len):
    positions = jnp.arange(seq_len, dtype=jnp.float32)
    inverse_freq = 10000.0 ** (-jnp.arange(HEAD_DIM // 2, dtype=jnp.float32) * 2.0 / HEAD_DIM)
    angles = positions[:, None] * inverse_freq[None, :]
    return (jnp.cos(angles)[:, None, :], jnp.sin(angles)[:, None, :])


def rotate(values, cosine, sine_vals):
    first_half = values[..., : HEAD_DIM // 2]
    second_half = values[..., HEAD_DIM // 2 :]
    return jnp.concatenate(
        [
            first_half * cosine - second_half * sine_vals,
            second_half * cosine + first_half * sine_vals,
        ],
        axis=-1,
    )


def rotate_back(values, cosine, sine_vals):
    first_half = values[..., : HEAD_DIM // 2]
    second_half = values[..., HEAD_DIM // 2 :]
    return jnp.concatenate(
        [
            first_half * cosine + second_half * sine_vals,
            second_half * cosine - first_half * sine_vals,
        ],
        axis=-1,
    )


def slot_tables(segment_row, route_row, experts_all, capacity):
    valid_tok = segment_row > 0
    flat_routes = route_row.reshape(-1)
    live_route = jnp.repeat(valid_tok, route_row.shape[1])
    route_onehot = (
        flat_routes[:, None] == jnp.arange(experts_all, dtype=jnp.int32)[None, :]
    ) & live_route[:, None]
    counts = jnp.cumsum(route_onehot.astype(jnp.int32), axis=0)
    ranking = jnp.sum(jnp.where(route_onehot, counts - 1, 0), axis=1)
    kept_mask = live_route & (ranking < capacity)
    dest_slot = jnp.where(kept_mask, flat_routes * capacity + ranking, experts_all * capacity)
    route_ids = jnp.arange(flat_routes.shape[0], dtype=jnp.int32)
    slot_route = (
        jnp.zeros((experts_all * capacity,), jnp.int32).at[dest_slot].set(route_ids, mode="drop")
    )
    slot_filled = (
        jnp.zeros((experts_all * capacity,), jnp.bool_).at[dest_slot].set(True, mode="drop")
    )
    return (kept_mask, dest_slot, slot_route, slot_filled)


def attention_scores(queries_b, keys_b, allowed):
    raw_scores = jnp.einsum(
        "sjgd,tjd->jgst", queries_b, keys_b, preferred_element_type=jnp.float32
    ) * HEAD_DIM ** (-0.5)
    return jnp.where(allowed, raw_scores, -1e30)


def reduce_grads(dense_part, expert_part):
    dense_sums = lax.psum_scatter(dense_part, ("dp", "expert"), scatter_dimension=0, tiled=True)
    expert_sums = (
        lax.psum_scatter(expert_part[0], "dp", scatter_dimension=1, tiled=True),
        lax.psum_scatter(expert_part[1], "dp", scatter_dimension=1, tiled=True),
    )
    return (dense_sums, expert_sums)


def on_device(
    tokens,
    segment_ids,
    routes,
    cotangent,
    attn_gain,
    query_weight,
    key_weight,
    value_weight,
    output_weight,
    expert_gain,
    router_weight,
    expert_in,
    expert_out,
):
    micro_count = tokens.shape[0]
    seq_len = tokens.shape[1]
    groups = lax.axis_size("expert")
    local_experts = expert_in.shape[0]
    experts_all = groups * local_experts
    capacity = seq_len * TOPK // experts_all
    group_heads = Q_HEADS // KV_HEADS
    cosine, sine_vals = rotary_tables(seq_len)
    positions = jnp.arange(seq_len)
    causal = positions[None, :] <= positions[:, None]
    dense_shards = (
        attn_gain,
        query_weight,
        key_weight,
        value_weight,
        output_weight,
        expert_gain,
        router_weight,
    )

    def fetch_dense():
        return (
            lax.all_gather(dense_shards[0], ("dp", "expert"), axis=0, tiled=True),
            lax.all_gather(dense_shards[1], ("dp", "expert"), axis=0, tiled=True),
            lax.all_gather(dense_shards[2], ("dp", "expert"), axis=0, tiled=True),
            lax.all_gather(dense_shards[3], ("dp", "expert"), axis=0, tiled=True),
            lax.all_gather(dense_shards[4], ("dp", "expert"), axis=0, tiled=True),
            lax.all_gather(dense_shards[5], ("dp", "expert"), axis=0, tiled=True),
            lax.all_gather(dense_shards[6], ("dp", "expert"), axis=0, tiled=True),
        )

    def fetch_experts():
        return (
            lax.all_gather(expert_in, "dp", axis=1, tiled=True),
            lax.all_gather(expert_out, "dp", axis=1, tiled=True),
        )

    def send_out(buffer):
        return lax.all_to_all(buffer, "expert", split_axis=0, concat_axis=0, tiled=True)

    def send_back(buffer):
        return lax.all_to_all(buffer, "expert", split_axis=0, concat_axis=0, tiled=True)

    dense_acc = tuple(
        (
            jnp.zeros(
                (shard_arr.shape[0] * lax.axis_size(("dp", "expert")),) + shard_arr.shape[1:],
                jnp.float32,
            )
            for shard_arr in dense_shards
        )
    )
    expert_acc = (
        jnp.zeros((local_experts, D, 2 * F), jnp.float32),
        jnp.zeros((local_experts, F, D), jnp.float32),
    )
    block_list = []
    grad_list = []
    for micro_step in range(micro_count):
        dense_full, experts_full = (fetch_dense(), fetch_experts())
        gain_one, query_full, key_full, value_full, output_full, gain_two, router_full = dense_full
        in_full, out_full = experts_full
        inputs = tokens[micro_step].astype(jnp.float32)
        segment_row = segment_ids[micro_step]
        route_row = routes[micro_step]
        valid_col = (segment_row > 0).astype(jnp.float32)[:, None]
        allowed = (segment_row[:, None] == segment_row[None, :]) & causal
        normed, norm_pull = jax.vjp(rms_forward, inputs, gain_one.astype(jnp.float32))
        normed_b = normed.astype(jnp.bfloat16)
        queries = jnp.dot(normed_b, query_full, preferred_element_type=jnp.float32).reshape(
            seq_len, Q_HEADS, HEAD_DIM
        )
        queries_b = (
            rotate(queries, cosine, sine_vals)
            .astype(jnp.bfloat16)
            .reshape(seq_len, KV_HEADS, group_heads, HEAD_DIM)
        )
        keys_raw = jnp.dot(normed_b, key_full, preferred_element_type=jnp.float32).reshape(
            seq_len, KV_HEADS, HEAD_DIM
        )
        keys_b = rotate(keys_raw, cosine, sine_vals).astype(jnp.bfloat16)
        values_b = (
            jnp.dot(normed_b, value_full, preferred_element_type=jnp.float32)
            .astype(jnp.bfloat16)
            .reshape(seq_len, KV_HEADS, HEAD_DIM)
        )
        scores = attention_scores(queries_b, keys_b, allowed)
        row_top = jnp.max(scores, axis=-1, keepdims=True)
        expo_vals = jnp.exp(scores - row_top)
        row_total = jnp.sum(expo_vals, axis=-1, keepdims=True)
        log_total = row_top + jnp.log(row_total)
        attn_probs = (expo_vals / row_total).astype(jnp.bfloat16)
        mixed_heads = jnp.einsum(
            "jgst,tjd->sjgd", attn_probs, values_b, preferred_element_type=jnp.float32
        )
        mixed_heads = mixed_heads.astype(jnp.bfloat16).reshape(seq_len, Q_HEADS * HEAD_DIM)
        attn_out = jnp.dot(mixed_heads, output_full, preferred_element_type=jnp.float32)
        residual = inputs + attn_out
        normed_two, norm_pull_two = jax.vjp(rms_forward, residual, gain_two.astype(jnp.float32))
        normed_two_b = normed_two.astype(jnp.bfloat16)
        logits = jnp.dot(normed_two_b, router_full, preferred_element_type=jnp.float32)
        route_hot = route_row[:, :, None] == jnp.arange(experts_all, dtype=jnp.int32)[None, None, :]
        chosen = jnp.sum(jnp.where(route_hot, logits[:, None, :], 0.0), axis=2)
        chosen_exp = jnp.exp(chosen - jnp.max(chosen, axis=1, keepdims=True))
        gate_vals = chosen_exp / jnp.sum(chosen_exp, axis=1, keepdims=True)
        kept_mask, dest_slot, slot_route, slot_filled = slot_tables(
            segment_row, route_row, experts_all, capacity
        )
        slot_token = slot_route // TOPK
        filled_col = slot_filled[:, None]
        dispatched = jnp.where(filled_col, jnp.take(normed_two_b, slot_token, axis=0), 0)
        received = send_out(dispatched.reshape(groups, local_experts, capacity, D))
        gate_up = jnp.einsum(
            "secd,edf->secf", received, in_full, preferred_element_type=jnp.float32
        )
        gate_part = gate_up[..., :F]
        up_part = gate_up[..., F:]
        sigmoid_gate = jax.nn.sigmoid(gate_part)
        hidden = (gate_part * sigmoid_gate * up_part).astype(jnp.bfloat16)
        expert_rows = jnp.einsum(
            "secf,efd->secd", hidden, out_full, preferred_element_type=jnp.float32
        ).astype(jnp.bfloat16)
        returned = send_back(expert_rows).reshape(experts_all * capacity, D)
        safe_slot = jnp.minimum(dest_slot, experts_all * capacity - 1)
        route_rows = jnp.take(returned, safe_slot, axis=0).reshape(seq_len, TOPK, D)
        kept_grid = kept_mask.reshape(seq_len, TOPK)
        weights_kept = gate_vals * kept_grid.astype(jnp.float32)
        mixture = jnp.sum(weights_kept[:, :, None] * route_rows.astype(jnp.float32), axis=1)
        block_list.append(((residual + mixture) * valid_col).astype(jnp.bfloat16))
        dense_full, experts_full = (fetch_dense(), fetch_experts())
        gain_one, query_full, key_full, value_full, output_full, gain_two, router_full = dense_full
        in_full, out_full = experts_full
        out_grad = cotangent[micro_step].astype(jnp.float32) * valid_col
        dweights = jnp.sum(route_rows.astype(jnp.float32) * out_grad[:, None, :], axis=2)
        dgate_vals = dweights * kept_grid.astype(jnp.float32)
        dchosen = gate_vals * (dgate_vals - jnp.sum(gate_vals * dgate_vals, axis=1, keepdims=True))
        dlogits = jnp.sum(jnp.where(route_hot, dchosen[:, :, None], 0.0), axis=1).astype(
            jnp.bfloat16
        )
        router_grad = jnp.einsum(
            "sd,se->de", normed_two_b, dlogits, preferred_element_type=jnp.float32
        )
        dnormed_two = jnp.einsum(
            "se,de->sd", dlogits, router_full, preferred_element_type=jnp.float32
        )
        slot_weight = jnp.take(weights_kept.reshape(-1), slot_route)
        dslot_rows = jnp.where(
            filled_col, slot_weight[:, None] * jnp.take(out_grad, slot_token, axis=0), 0.0
        ).astype(jnp.bfloat16)
        dreceived = send_out(dslot_rows.reshape(groups, local_experts, capacity, D))
        dhidden = jnp.einsum(
            "secd,efd->secf", dreceived, out_full, preferred_element_type=jnp.float32
        )
        silu_grad = sigmoid_gate * (1.0 + gate_part * (1.0 - sigmoid_gate))
        dgate_up = jnp.concatenate(
            [dhidden * up_part * silu_grad, dhidden * gate_part * sigmoid_gate], axis=-1
        ).astype(jnp.bfloat16)
        grad_out_w = jnp.einsum(
            "secf,secd->efd", hidden, dreceived, preferred_element_type=jnp.float32
        )
        grad_in_w = jnp.einsum(
            "secd,secf->edf", received, dgate_up, preferred_element_type=jnp.float32
        )
        dslot_in = jnp.einsum(
            "secf,edf->secd", dgate_up, in_full, preferred_element_type=jnp.float32
        ).astype(jnp.bfloat16)
        dreturned = send_back(dslot_in).reshape(experts_all * capacity, D)
        droute = jnp.take(dreturned, safe_slot, axis=0).reshape(seq_len, TOPK, D)
        dnormed_two = dnormed_two + jnp.sum(
            jnp.where(kept_grid[:, :, None], droute.astype(jnp.float32), 0.0), axis=1
        )
        dresid_norm, dgain_two = norm_pull_two(dnormed_two)
        dresid = out_grad + dresid_norm
        dattn_b = dresid.astype(jnp.bfloat16)
        grad_output_w = jnp.einsum(
            "sq,sd->qd", mixed_heads, dattn_b, preferred_element_type=jnp.float32
        )
        dmixed = jnp.einsum("sd,qd->sq", dattn_b, output_full, preferred_element_type=jnp.float32)
        dmixed = dmixed.astype(jnp.bfloat16).reshape(seq_len, KV_HEADS, group_heads, HEAD_DIM)
        scores = attention_scores(queries_b, keys_b, allowed)
        attn_exact = jnp.exp(scores - log_total)
        dprob_vals = jnp.einsum(
            "sjgd,tjd->jgst", dmixed, values_b, preferred_element_type=jnp.float32
        )
        dvalues = jnp.einsum(
            "jgst,sjgd->tjd",
            attn_exact.astype(jnp.bfloat16),
            dmixed,
            preferred_element_type=jnp.float32,
        )
        dscore = (
            attn_exact * (dprob_vals - jnp.sum(attn_exact * dprob_vals, axis=-1, keepdims=True))
        ).astype(jnp.bfloat16)
        dqueries = jnp.einsum(
            "jgst,tjd->sjgd", dscore, keys_b, preferred_element_type=jnp.float32
        ) * HEAD_DIM ** (-0.5)
        dkeys_rot = jnp.einsum(
            "jgst,sjgd->tjd", dscore, queries_b, preferred_element_type=jnp.float32
        ) * HEAD_DIM ** (-0.5)
        dquery_raw = (
            rotate_back(dqueries.reshape(seq_len, Q_HEADS, HEAD_DIM), cosine, sine_vals)
            .reshape(seq_len, Q_HEADS * HEAD_DIM)
            .astype(jnp.bfloat16)
        )
        dkey_raw = (
            rotate_back(dkeys_rot, cosine, sine_vals)
            .reshape(seq_len, KV_HEADS * HEAD_DIM)
            .astype(jnp.bfloat16)
        )
        dvalue_raw = dvalues.astype(jnp.bfloat16).reshape(seq_len, KV_HEADS * HEAD_DIM)
        grad_query_w = jnp.einsum(
            "sd,sq->dq", normed_b, dquery_raw, preferred_element_type=jnp.float32
        )
        grad_key_w = jnp.einsum("sd,sq->dq", normed_b, dkey_raw, preferred_element_type=jnp.float32)
        grad_value_w = jnp.einsum(
            "sd,sq->dq", normed_b, dvalue_raw, preferred_element_type=jnp.float32
        )
        dnormed = jnp.einsum(
            "sq,dq->sd", dquery_raw, query_full, preferred_element_type=jnp.float32
        )
        dnormed = dnormed + jnp.einsum(
            "sq,dq->sd", dkey_raw, key_full, preferred_element_type=jnp.float32
        )
        dnormed = dnormed + jnp.einsum(
            "sq,dq->sd", dvalue_raw, value_full, preferred_element_type=jnp.float32
        )
        dinputs_norm, dgain_one = norm_pull(dnormed)
        grad_list.append((dresid + dinputs_norm).astype(jnp.bfloat16))
        dense_part = (
            dgain_one,
            grad_query_w,
            grad_key_w,
            grad_value_w,
            grad_output_w,
            dgain_two,
            router_grad,
        )
        expert_part = (grad_in_w, grad_out_w)
        dense_acc = tuple(
            (acc_item + part_item for acc_item, part_item in zip(dense_acc, dense_part))
        )
        expert_acc = tuple(
            (acc_item + part_item for acc_item, part_item in zip(expert_acc, expert_part))
        )
    dense_acc, expert_acc = reduce_grads(dense_acc, expert_acc)
    block_out = jnp.stack(block_list, axis=0)
    token_grad = jnp.stack(grad_list, axis=0)
    return (
        block_out,
        token_grad,
        dense_acc[0],
        dense_acc[1],
        dense_acc[2],
        dense_acc[3],
        dense_acc[4],
        dense_acc[5],
        dense_acc[6],
        expert_acc[0],
        expert_acc[1],
    )


def solution(mesh):
    in_specs = (
        P(("dp", "expert"), None, None),
        P(("dp", "expert"), None),
        P(("dp", "expert"), None, None),
        P(("dp", "expert"), None, None),
        P(("dp", "expert")),
        P(("dp", "expert"), None),
        P(("dp", "expert"), None),
        P(("dp", "expert"), None),
        P(("dp", "expert"), None),
        P(("dp", "expert")),
        P(("dp", "expert"), None),
        P("expert", "dp", None),
        P("expert", "dp", None),
    )
    out_specs = (
        P(("dp", "expert"), None, None),
        P(("dp", "expert"), None, None),
        P(("dp", "expert")),
        P(("dp", "expert"), None),
        P(("dp", "expert"), None),
        P(("dp", "expert"), None),
        P(("dp", "expert"), None),
        P(("dp", "expert")),
        P(("dp", "expert"), None),
        P("expert", "dp", None),
        P("expert", "dp", None),
    )
    return jax.shard_map(
        on_device, mesh=mesh, in_specs=in_specs, out_specs=out_specs, check_vma=False
    )
```

profile of v0, /device:TPU:1, one launch (start us, length us, event | category | flops | bytes accessed | tf_op | source)
XLA Modules:
  0.0 3501.7 jit_solution(16698553304973893116)
XLA Ops:
  17.1 68.9 %all-reduce.15 = (bf16[1536]{0:T(1024)(128)(2,1)S(1)}, bf16[1536]{0:T(1024)(128)(2,1)S(1)}) all-reduce(bf16[1536]{0:T(1024)(128)(2,1)S(1)} %dynamic-update-slice, bf16[1536]{0:T(1024)(128)(2,1)S(1)} %dynamic-update-slice.1), channel_id=1, replica_groups=mesh['dp'=64,'expert'=2] {'dp','expert'}, use_global_device_ids=true, to_apply=%add | all-reduce | flops 3072 | bytes 12288
  90.1 310.8 %all-gather.4 = bf16[128,12,16]{2,1,0:T(8,128)(2,1)S(1)} all-gather(bf16[1,12,16]{2,1,0:T(8,128)(2,1)} %bitcast.475), channel_id=1, replica_groups=mesh['dp'=64,'expert'=2] {'dp','expert'}, dimensions={0}, use_global_device_ids=true | all-gather | bytes 49536 | tf_op jit(solution)/shard_map/all_gather | solution.py:133
  420.5 195.9 %all-gather.16.cloned.1.call-done = bf16[128,12,512]{2,1,0:T(8,128)(2,1)} async-done(((bf16[1,12,512]{2,1,0:T(8,128)(2,1)}), bf16[128,12,512]{2,1,0:T(8,128)(2,1)}) %all-gather.16.cloned.1.call-update) | async-done | bytes 1572880 | tf_op jit(solution)/shard_map/all_gather | solution.py:130
  623.8 306.4 %all-gather.20.cloned.1.call-done = bf16[128,12,1536]{2,1,0:T(8,128)(2,1)} async-done(((bf16[1,12,1536]{2,1,0:T(8,128)(2,1)}), bf16[128,12,1536]{2,1,0:T(8,128)(2,1)}) %all-gather.20.cloned.1.call-update) | async-done | bytes 4718608 | tf_op jit(solution)/shard_map/all_gather | solution.py:128
  952.8 290.9 %all-gather.22.cloned.1.call-done = bf16[128,12,1536]{2,1,0:T(8,128)(2,1)} async-done(((bf16[1,12,1536]{2,1,0:T(8,128)(2,1)}), bf16[128,12,1536]{2,1,0:T(8,128)(2,1)}) %all-gather.22.cloned.1.call-update) | async-done | bytes 4718608 | tf_op jit(solution)/shard_map/all_gather | solution.py:131
  1285.7 95.7 %all-gather.12.cloned.1.call-done = bf16[8,1536,1024]{2,1,0:T(8,128)(2,1)} async-done(((bf16[8,24,1024]{2,1,0:T(8,128)(2,1)}), bf16[8,1536,1024]{2,1,0:T(8,128)(2,1)}) %all-gather.12.cloned.1.call-update) | async-done | bytes 25165840 | tf_op jit(solution)/shard_map/all_gather | solution.py:138
  1394.3 81.7 %all-gather.14.cloned.1.call-done = bf16[8,512,1536]{2,1,0:T(8,128)(2,1)} async-done(((bf16[8,8,1536]{2,1,0:T(8,128)(2,1)}), bf16[8,512,1536]{2,1,0:T(8,128)(2,1)}) %all-gather.14.cloned.1.call-update) | async-done | bytes 12582928 | tf_op jit(solution)/shard_map/all_gather | solution.py:139
  1491.6 15.4 all-to-all-done.1
  1527.7 15.2 all-to-all-done.4
  1552.4 12.9 fusion.48
  1608.0 13.0 all-to-all-done.2
  1645.1 15.0 all-to-all-done.3
  1676.3 13.3 fusion.67
  1690.7 16.8 bitcast_add_fusion.1
  1709.1 22.3 fusion.91
  1742.7 37.4 %bitcast_add_fusion = f32[8,1536,1024]{2,1,0:T(8,128)} fusion(f32[8,1536,1024,1]{2,1,0,3:T(8,128)} %fusion.91, bf16[2,8,32,1536]{3,2,1,0:T(8,128)(2,1)S(1)} %copy-done.18, bf16[2,8,32,512]{3,2,0,1:T(8,128)(2,1)} %get-tuple-element.66, bf16[2,8,32,512]{3,2,0,1:T(8,128)(2,1)S(1)} %get-tuple-element.65), kind=kOutput, calls=%fused_computation.14 | convolution fusion | flops 1625292800 | bytes 103284736 | tf_op jit(solution)/shard_map/secd,secf->edf/dot_general | solution.py:265
  1781.4 13.9 fusion.45
  1854.9 904.6 %fusion.226 = (f32[16,1536]{1,0:T(8,128)}, f32[16,512]{1,0:T(8,128)}, f32[16,512]{1,0:T(8,128)}, f32[16,1536]{1,0:T(8,128)}, f32[16,16]{1,0:T(8,128)S(1)}) fusion(f32[1536,1536]{1,0:T(8,128)} %convolution_add_fusion.1, f32[1536,512]{1,0:T(8,128)S(1)} %convolution_add_fusion.3, f32[1536,512]{1,0:T(8,128)} %convolution_add_fusion.2, ...), kind=kCustom, calls=%all-reduce-scatter.5 | all-reduce-scatter fusion | flops 8421377 | bytes 25527296
  3217.9 62.0 %all-reduce.14 = (f32[1536]{0:T(1024)S(1)}, f32[1536]{0:T(1024)S(1)}) all-reduce(f32[1536]{0:T(1024)S(1)} %add.295, f32[1536]{0:T(1024)S(1)} %add.300), channel_id=2, replica_groups=mesh['dp'=64,'expert'=2] {'dp','expert'}, use_global_device_ids=true, to_apply=%region_42.47.clone | all-reduce | flops 3072 | bytes 24576
  3281.0 23.2 concatenate.64
  3325.2 20.2 concatenate.61
  3345.4 25.9 concatenate.62
  3408.1 31.8 concatenate.60
  3440.0 52.4 %concatenate.63 = f32[524,1536]{1,0:T(8,128)} concatenate(f32[12,1536]{1,0:T(8,128)S(1)} %copy-done.103, f32[16,1536]{1,0:T(8,128)} %copy-done.134, f32[16,1536]{1,0:T(8,128)} %copy-done.137, f32[16,1536]{1,0:T(8,128)} %copy-done.138, f32[16,1536]{1,0:T(8,128)} %copy-done.139, f32[16,1536]{1,0:T(8,128)} %copy-done.140, f32[16,1536]{1,0:T(8,128)} %copy-done.141, ...), dimensions={0} | concatenate | bytes 6438912
  (1191 shorter events, 834.9 us)
Async XLA Ops:
  7.2 409.2 %all-gather.18.cloned.1.call-start = ((), (), s32[]{:S(2)}) async-start(), calls=%async_computation.15 | async-start | bytes 2113536 | tf_op jit(solution)/shard_map/all_gather | solution.py:129
  7.9 608.5 %all-gather.16.cloned.1.call-start = ((), (), s32[]{:S(2)}) async-start(), calls=%async_computation.14 | async-start | bytes 2113536 | tf_op jit(solution)/shard_map/all_gather | solution.py:130
  8.7 921.4 %all-gather.20.cloned.1.call-start = ((), (), s32[]{:S(2)}) async-start(), calls=%async_computation.16 | async-start | bytes 6340608 | tf_op jit(solution)/shard_map/all_gather | solution.py:128
  9.4 1234.3 %all-gather.22.cloned.1.call-start = ((), (), s32[]{:S(2)}) async-start(), calls=%async_computation.17 | async-start | bytes 6340608 | tf_op jit(solution)/shard_map/all_gather | solution.py:131
  10.0 1371.4 %all-gather.12.cloned.1.call-start = ((), (), s32[]{:S(2)}) async-start(), calls=%async_computation.10 | async-start | bytes 25559040 | tf_op jit(solution)/shard_map/all_gather | solution.py:138
  10.6 1465.4 %all-gather.14.cloned.1.call-start = ((), (), s32[]{:S(2)}) async-start(), calls=%async_computation.11 | async-start | bytes 12779520 | tf_op jit(solution)/shard_map/all_gather | solution.py:139
  1676.2 1818.3 %reduce-scatter.15.cloned.1.call-start = ((), (), s32[]{:S(2)}) async-start(), calls=%async_computation.13 | async-start | bytes 25559040 | tf_op jit(solution)/shard_map/reduce_scatter | solution.py:85
  1707.6 1787.0 %reduce-scatter.13.cloned.1.call-start = ((), (), s32[]{:S(2)}) async-start(), calls=%async_computation.12 | async-start | bytes 51118080 | tf_op jit(solution)/shard_map/reduce_scatter | solution.py:84
  2759.6 171.7 %collective-permute-start.62 = (f32[16,512]{1,0:T(8,128)}, f32[16,512]{1,0:T(8,128)S(1)}, u32[]{:S(2)}, u32[]{:S(2)}) collective-permute-start(f32[16,512]{1,0:T(8,128)} %get-tuple-element.43), channel_id=1, source_target_pairs={{0,31},{1,32},{2,33},{3,34},{4,35},{5,36},{6,37},{7,38},{8,39},{9,... | collective-permute-start | bytes 98312
  2761.6 166.9 %collective-permute-start.63 = (f32[12,512]{1,0:T(8,128)S(1)}, f32[12,512]{1,0:T(8,128)S(1)}, u32[]{:S(2)}, u32[]{:S(2)}) collective-permute-start(f32[12,512]{1,0:T(8,128)S(1)} %slice.171), channel_id=1, source_target_pairs={{0,32},{1,33},{2,34},{3,35},{4,36},{5,37},{6,38},{7,39},{8,40},{9,... | collective-permute-start | bytes 73736
  2763.7 166.2 %collective-permute-start.95 = (f32[12,512]{1,0:T(8,128)S(1)}, f32[12,512]{1,0:T(8,128)S(1)}, u32[]{:S(2)}, u32[]{:S(2)}) collective-permute-start(f32[12,512]{1,0:T(8,128)S(1)} %slice.172), channel_id=1, source_target_pairs={{0,32},{1,33},{2,34},{3,35},{4,36},{5,37},{6,38},{7,39},{8,40},{9,... | collective-permute-start | bytes 73736
  3205.5 98.8 %collective-permute-start.115 = (f32[16,1536]{1,0:T(8,128)S(1)}, f32[16,1536]{1,0:T(8,128)S(1)}, u32[]{:S(2)}, u32[]{:S(2)}) collective-permute-start(f32[16,1536]{1,0:T(8,128)S(1)} %copy-done.71), channel_id=1, source_target_pairs={{0,20},{1,21},{2,22},{3,23},{4,24},{5,25},{6,26},{7,27},{8,28},{9,... | collective-permute-start | bytes 294920
  3206.8 102.0 %collective-permute-start.114 = (f32[16,1536]{1,0:T(8,128)S(1)}, f32[16,1536]{1,0:T(8,128)S(1)}, u32[]{:S(2)}, u32[]{:S(2)}) collective-permute-start(f32[16,1536]{1,0:T(8,128)S(1)} %copy-done.71), channel_id=1, source_target_pairs={{0,19},{1,20},{2,21},{3,22},{4,23},{5,24},{6,25},{7,26},{8,27},{9,... | collective-permute-start | bytes 294920
  3208.5 104.1 %collective-permute-start.113 = (f32[16,1536]{1,0:T(8,128)S(1)}, f32[16,1536]{1,0:T(8,128)S(1)}, u32[]{:S(2)}, u32[]{:S(2)}) collective-permute-start(f32[16,1536]{1,0:T(8,128)S(1)} %copy-done.71), channel_id=1, source_target_pairs={{0,18},{1,19},{2,20},{3,21},{4,22},{5,23},{6,24},{7,25},{8,26},{9,... | collective-permute-start | bytes 294920
  3210.7 105.0 %collective-permute-start.112 = (f32[16,1536]{1,0:T(8,128)S(1)}, f32[16,1536]{1,0:T(8,128)S(1)}, u32[]{:S(2)}, u32[]{:S(2)}) collective-permute-start(f32[16,1536]{1,0:T(8,128)S(1)} %copy-done.71), channel_id=1, source_target_pairs={{0,17},{1,18},{2,19},{3,20},{4,21},{5,22},{6,23},{7,24},{8,25},{9,... | collective-permute-start | bytes 294920
  3213.4 105.3 %collective-permute-start.111 = (f32[16,1536]{1,0:T(8,128)S(1)}, f32[16,1536]{1,0:T(8,128)S(1)}, u32[]{:S(2)}, u32[]{:S(2)}) collective-permute-start(f32[16,1536]{1,0:T(8,128)S(1)} %copy-done.71), channel_id=1, source_target_pairs={{0,16},{1,17},{2,18},{3,19},{4,20},{5,21},{6,22},{7,23},{8,24},{9,... | collective-permute-start | bytes 294920
  3304.3 67.0 %collective-permute-start.110 = (f32[16,1536]{1,0:T(8,128)S(1)}, f32[16,1536]{1,0:T(8,128)}, u32[]{:S(2)}, u32[]{:S(2)}) collective-permute-start(f32[16,1536]{1,0:T(8,128)S(1)} %copy-done.71), channel_id=1, source_target_pairs={{0,15},{1,16},{2,17},{3,18},{4,19},{5,20},{6,21},{7,22},{8,23},{9,... | collective-permute-start | bytes 294920
  3308.7 64.9 %collective-permute-start.109 = (f32[16,1536]{1,0:T(8,128)S(1)}, f32[16,1536]{1,0:T(8,128)}, u32[]{:S(2)}, u32[]{:S(2)}) collective-permute-start(f32[16,1536]{1,0:T(8,128)S(1)} %copy-done.71), channel_id=1, source_target_pairs={{0,14},{1,15},{2,16},{3,17},{4,18},{5,19},{6,20},{7,21},{8,22},{9,... | collective-permute-start | bytes 294920
  3312.6 64.9 %collective-permute-start.108 = (f32[16,1536]{1,0:T(8,128)S(1)}, f32[16,1536]{1,0:T(8,128)}, u32[]{:S(2)}, u32[]{:S(2)}) collective-permute-start(f32[16,1536]{1,0:T(8,128)S(1)} %copy-done.71), channel_id=1, source_target_pairs={{0,13},{1,14},{2,15},{3,16},{4,17},{5,18},{6,19},{7,20},{8,21},{9,... | collective-permute-start | bytes 294920
  3315.7 66.1 %collective-permute-start.107 = (f32[16,1536]{1,0:T(8,128)S(1)}, f32[16,1536]{1,0:T(8,128)}, u32[]{:S(2)}, u32[]{:S(2)}) collective-permute-start(f32[16,1536]{1,0:T(8,128)S(1)} %copy-done.71), channel_id=1, source_target_pairs={{0,12},{1,13},{2,14},{3,15},{4,16},{5,17},{6,18},{7,19},{8,20},{9,... | collective-permute-start | bytes 294920
  3318.7 69.0 %collective-permute-start.106 = (f32[16,1536]{1,0:T(8,128)S(1)}, f32[16,1536]{1,0:T(8,128)}, u32[]{:S(2)}, u32[]{:S(2)}) collective-permute-start(f32[16,1536]{1,0:T(8,128)S(1)} %copy-done.71), channel_id=1, source_target_pairs={{0,11},{1,12},{2,13},{3,14},{4,15},{5,16},{6,17},{7,18},{8,19},{9,... | collective-permute-start | bytes 294920
  3391.3 48.6 %collective-permute-start.100 = (f32[16,1536]{1,0:T(8,128)S(1)}, f32[16,1536]{1,0:T(8,128)}, u32[]{:S(2)}, u32[]{:S(2)}) collective-permute-start(f32[16,1536]{1,0:T(8,128)S(1)} %copy-done.71), channel_id=1, source_target_pairs={{0,5},{1,6},{2,7},{3,8},{4,9},{5,10},{6,11},{7,12},{8,13},{9,14},{... | collective-permute-start | bytes 294920
  3393.8 46.1 %collective-permute-start.99 = (f32[16,1536]{1,0:T(8,128)S(1)}, f32[16,1536]{1,0:T(8,128)}, u32[]{:S(2)}, u32[]{:S(2)}) collective-permute-start(f32[16,1536]{1,0:T(8,128)S(1)} %copy-done.71), channel_id=1, source_target_pairs={{0,4},{1,5},{2,6},{3,7},{4,8},{5,9},{6,10},{7,11},{8,12},{9,13},{1... | collective-permute-start | bytes 294920
  3399.2 40.8 %collective-permute-start.98 = (f32[16,1536]{1,0:T(8,128)S(1)}, f32[16,1536]{1,0:T(8,128)}, u32[]{:S(2)}, u32[]{:S(2)}) collective-permute-start(f32[16,1536]{1,0:T(8,128)S(1)} %copy-done.71), channel_id=1, source_target_pairs={{0,3},{1,4},{2,5},{3,6},{4,7},{5,8},{6,9},{7,10},{8,11},{9,12},{10... | collective-permute-start | bytes 294920
  (457 other events, 24066.4 us)
Sparse Core Ops, SparseCore 0:
  9.7 303.6 all-gather.17
  315.1 301.2 all-gather.15
  618.1 311.9 all-gather.19
  931.7 311.9 all-gather.21
  1246.8 134.4 all-gather.11
  1384.5 91.3 all-gather.13
  1707.7 272.2 reduce-scatter.14
  1988.1 489.7 reduce-scatter.12
where the time goes:
time: 3520 us; the launch traced here: 3500 us
  blocking collectives  1350 us (38%)
  waiting for transfers between devices  1070 us (30%)
  starting transfers between devices  519 us (15%)
  local copies, waits for them, and re-layouts  263 us (7%)
  matrix products  233 us (7%)
  other arithmetic  48.5 us (1%)
    unnamed x3, blocking collectives  1040 us
    unnamed x160, starting transfers between devices  487 us
    all_gather x1, blocking collectives, fetch_dense(): lax.all_gather(dense_shards[6], ('dp', 'expert'), axis=0, tiled=True)  311 us
    all_gather x1, waiting for transfers between devices, fetch_dense(): lax.all_gather(dense_shards[1], ('dp', 'expert'), axis=0, tiled=True)  306 us
    all_gather x1, waiting for transfers between devices, fetch_dense(): lax.all_gather(dense_shards[4], ('dp', 'expert'), axis=0, tiled=True)  291 us
    unnamed x636, local copies, waits for them, and re-layouts  197 us
    all_gather x1, waiting for transfers between devices, fetch_dense(): lax.all_gather(dense_shards[3], ('dp', 'expert'), axis=0, tiled=True)  196 us
    all_gather x1, waiting for transfers between devices, fetch_experts(): lax.all_gather(expert_in, 'dp', axis=1, tiled=True)  95.7 us
  transfers between devices with their start and end apart: 176, of which 15 were waited for; matrix products, arithmetic and copies ran while one was open for 38% of the time, Pallas kernels for 0%

commit v1 on v0

v1 whole, which is shorter than its diff:
```python
import functools

import jax
import jax.numpy as jnp
import numpy as np
from jax import lax
from jax.experimental import pallas as pl
from jax.experimental.pallas import tpu as pltpu
from jax.sharding import Mesh
from jax.sharding import PartitionSpec as P

D = 1536
Q_HEADS = 24
KV_HEADS = 8
HEAD_DIM = 64
F = 512
TOPK = 8
EXPERTS = 16
SEQ = 64
CAP = 32

AX = ("z", "yh", "x", "c", "yl")
DIMS = (4, 2, 4, 2, 2)
EPS = 1e-5
NEG = -1e30
TOK = 128
EXT = 144
QKV = 1280
QKVM = 1408
HQ = 768
HK = 256
bf16 = jnp.bfloat16
f32 = jnp.float32


def coords_list():
    return list(np.ndindex(*DIMS))


def send(value, dz=0, dh=0, dx=0, dc=0, dl=0):
    flat = {pos: i for i, pos in enumerate(coords_list())}
    pairs = [
        (i, flat[(z ^ dz, h ^ dh, x ^ dx, c ^ dc, l ^ dl)])
        for (z, h, x, c, l), i in flat.items()
    ]
    return lax.ppermute(value, AX, pairs)


def dot(a, b):
    return jnp.dot(a, b, preferred_element_type=f32)


def dot_t(a, b):
    return lax.dot_general(a, b, (((1,), (1,)), ((), ())), preferred_element_type=f32)


def t_dot(a, b):
    return lax.dot_general(a, b, (((0,), (0,)), ((), ())), preferred_element_type=f32)


def params(mib=60):
    return pltpu.CompilerParams(vmem_limit_bytes=mib * 2**20)


def rope_tables():
    angle = np.arange(SEQ)[:, None] * (10000.0 ** (-np.arange(32) * 2.0 / 64))[None, :]
    cosine, sine = np.cos(angle), np.sin(angle)
    cos_full = np.concatenate([cosine, cosine] * 2, axis=1)
    sin_full = np.concatenate([-sine, sine] * 2, axis=1)
    return np.tile(cos_full, (4, 1)).astype(np.float32), np.tile(sin_full, (4, 1)).astype(np.float32)


def turn(values, cos_full, sin_full):
    width = values.shape[1]
    lane = lax.broadcasted_iota(jnp.int32, values.shape, 1)
    ahead = pltpu.roll(values, width - 32, 1)
    behind = pltpu.roll(values, 32, 1)
    partner = jnp.where((lane % 64) < 32, ahead, behind)
    copies = width // 128
    cos_wide = jnp.concatenate([cos_full] * copies, axis=1)
    sin_wide = jnp.concatenate([sin_full] * copies, axis=1)
    return values * cos_wide + partner * sin_wide


def allowed_mask(ints):
    row = jnp.broadcast_to(ints[8:9, :], (TOK, TOK))
    col = row.T
    p = lax.broadcasted_iota(jnp.int32, (TOK, TOK), 0)
    t = lax.broadcasted_iota(jnp.int32, (TOK, TOK), 1)
    return (row == col) & (t <= p) & ((p < SEQ) == (t < SEQ))


def piece_copies(pieces, target, sems, z, x):
    copies = []
    for j in range(4):
        for k in range(4):
            for h in range(2):
                start = pl.multiple_of((((z ^ j) * 2 + h) * 4 + (x ^ k)) * 48, 16)
                copies.append(
                    pltpu.make_async_copy(
                        pieces[j * 4 + k].at[pl.ds(48 * h, 48), :],
                        target.at[pl.ds(start, 48), :],
                        sems.at[(j * 4 + k) * 2 + h],
                    )
                )
    return copies


def o_copies(pieces, target, sems, z, x):
    copies = []
    for j in range(4):
        for k in range(4):
            start = pl.multiple_of(((z ^ j) * 4 + (x ^ k)) * 48, 16)
            copies.append(
                pltpu.make_async_copy(
                    pieces[j * 4 + k], target.at[pl.ds(start, 48), :], sems.at[j * 4 + k]
                )
            )
    return copies


def spec_any():
    return pl.BlockSpec(memory_space=pl.ANY)


def spec_vmem():
    return pl.BlockSpec(memory_space=pltpu.VMEM)


def spec_smem():
    return pl.BlockSpec(memory_space=pltpu.SMEM)


def kernel_attn(where, xo, xs, cos_ref, sin_ref, *rest):
    pieces = rest[:16]
    normed_ref, q_ref, k_ref, v_ref, mixed_ref, misc_ref = rest[16:22]
    w, sems = rest[22:]
    copies = piece_copies(pieces, w, sems, where[0], where[2])
    for item in copies:
        item.start()
    xin = jnp.concatenate([xo[:TOK, :], xs[:TOK, :]], axis=0).astype(f32)
    rinv = lax.rsqrt(jnp.mean(xin * xin, axis=1, keepdims=True) + EPS)
    for item in copies:
        item.wait()
    eye = (
        lax.broadcasted_iota(jnp.int32, (128, 128), 0) == lax.broadcasted_iota(jnp.int32, (128, 128), 1)
    ).astype(f32).astype(bf16)
    misc = dot_t(eye, w[:, QKV:])
    misc_ref[...] = misc.astype(bf16)
    normed = (xin * rinv * misc[16:17, :]).astype(bf16)
    normed_ref[...] = normed
    cos_full, sin_full = cos_ref[...], sin_ref[...]
    qf = dot(normed, w[:, :HQ])
    q_ref[...] = turn(qf, cos_full, sin_full).astype(bf16)
    kf = dot(normed, w[:, HQ : HQ + HK])
    k_ref[...] = turn(kf, cos_full, sin_full).astype(bf16)
    v_ref[...] = dot(normed, w[:, HQ + HK : QKV]).astype(bf16)
    for part, src in enumerate((xo, xs)):
        ok = allowed_mask(src[TOK:EXT, :TOK].astype(f32))
        ok3 = jnp.concatenate([ok.astype(f32)] * 3, axis=0) > 0.5
        rows = slice(part * TOK, (part + 1) * TOK)
        for a in range(4):
            keys = k_ref[rows, a * 64 : (a + 1) * 64]
            vals = v_ref[rows, a * 64 : (a + 1) * 64]
            q3 = jnp.concatenate(
                [q_ref[rows, (3 * a + g) * 64 : (3 * a + g + 1) * 64] for g in range(3)], axis=0
            )
            scores = jnp.where(ok3, dot_t(q3, keys) * 0.125, NEG)
            top = jnp.max(scores, axis=1, keepdims=True)
            expo = jnp.exp(scores - top)
            probs = (expo / jnp.sum(expo, axis=1, keepdims=True)).astype(bf16)
            out = dot(probs, vals).astype(bf16)
            for g in range(3):
                mixed_ref[rows, (3 * a + g) * 64 : (3 * a + g + 1) * 64] = out[
                    g * TOK : (g + 1) * TOK, :
                ]


def kernel_oproj(where, mixed_ref, *rest):
    pieces = rest[:16]
    own_ref, sib_ref, w, sems = rest[16:]
    copies = o_copies(pieces, w, sems, where[0], where[2])
    for item in copies:
        item.start()
    for item in copies:
        item.wait()
    out = dot(mixed_ref[...], w[...])
    own_ref[...] = out[:TOK, :]
    sib_ref[...] = out[TOK:, :]


def chosen_gates(misc, n2, ints):
    logits = dot_t(misc, n2)
    expert = lax.broadcasted_iota(jnp.int32, logits.shape, 0).astype(f32)
    hot = jnp.zeros(logits.shape, f32)
    for k in range(TOPK):
        hot = jnp.maximum(hot, (expert == ints[k : k + 1, :]).astype(f32))
    masked = jnp.where(hot > 0.5, logits, NEG)
    expo = jnp.where(hot > 0.5, jnp.exp(masked - jnp.max(masked, axis=0, keepdims=True)), 0.0)
    return expo / jnp.sum(expo, axis=0, keepdims=True)


def kernel_resid(xo, own_ref, recv_ref, misc_ref, resid_ref, n2_ref, gates_ref):
    resid = xo[:TOK, :].astype(f32) + own_ref[...] + recv_ref[...]
    resid_ref[...] = resid
    rinv = lax.rsqrt(jnp.mean(resid * resid, axis=1, keepdims=True) + EPS)
    n2 = (resid * rinv * misc_ref[17:18, :].astype(f32)).astype(bf16)
    n2_ref[...] = n2
    gates_ref[...] = chosen_gates(misc_ref[0:16, :], n2, xo[TOK:EXT, :TOK].astype(f32))


def kernel_expert(where, misc_ref, *rest):
    n2_in = rest[:16]
    gx_in = rest[16:32]
    w_in = rest[32:40]
    dn_own, dn_sib, mix_own, mix_sib = rest[40:44]
    wg_out = rest[44:52]
    (n2, gx, win, wout, disp, dslot, hid, dgu, gate_s, slot_s, hit_s, obuf, mbuf, wg,
     n2_sem, gx_sem, w_sem, o_sem, g_sem) = rest[52:]
    z, h, x, c, l = where[0], where[1], where[2], where[3], where[4]
    me = (l * 8 + x * 2 + c).astype(f32)
    w_copies = []
    for j in range(4):
        for b in range(2):
            m = j * 2 + b
            blk = (z ^ j) * 2 + (h ^ b)
            w_copies.append(
                pltpu.make_async_copy(
                    w_in[m].at[:, pl.ds(0, 1024)],
                    win.at[pl.ds(pl.multiple_of(blk * 192, 64), 192), :],
                    w_sem.at[m * 4],
                )
            )
            for t in range(3):
                w_copies.append(
                    pltpu.make_async_copy(
                        w_in[m].at[pl.ds(64 * t, 64), pl.ds(1024, 512)],
                        wout.at[pl.ds(pl.multiple_of(blk * 64, 64), 64), pl.ds(512 * t, 512)],
                        w_sem.at[m * 4 + 1 + t],
                    )
                )
    n2_copies = [
        pltpu.make_async_copy(n2_in[m], n2.at[pl.ds(TOK * m, TOK), :], n2_sem.at[m]) for m in range(16)
    ]
    gx_copies = [pltpu.make_async_copy(gx_in[m], gx.at[m], gx_sem.at[m]) for m in range(16)]
    for item in gx_copies + n2_copies + w_copies:
        item.start()
    for item in gx_copies + n2_copies:
        item.wait()
    token = lax.broadcasted_iota(jnp.int32, (TOK, TOK), 0)
    after = lax.broadcasted_iota(jnp.int32, (TOK, TOK), 1)
    before = ((token < after) & ((token < SEQ) == (after < SEQ))).astype(f32).astype(bf16)
    router = misc_ref[0:16, :]
    for m in range(16):
        ints = gx[m, TOK:EXT, :TOK].astype(f32)
        gates = chosen_gates(router, n2[TOK * m : TOK * (m + 1), :], ints)
        expert = lax.broadcasted_iota(jnp.int32, gates.shape, 0).astype(f32)
        gate_s[m : m + 1, :] = jnp.sum(jnp.where(expert == me, gates, 0.0), axis=0, keepdims=True)
        hit = jnp.max((ints[0:8, :] == me).astype(f32), axis=0, keepdims=True)
        hit_s[m : m + 1, :] = hit * (ints[8:9, :] > 0.5).astype(f32)
    hit = hit_s[...]
    rank = dot(hit.astype(bf16), before)
    lane = lax.broadcasted_iota(jnp.int32, (16, TOK), 1)
    kept = (hit > 0.5) & (rank < CAP - 0.5)
    slot_s[...] = jnp.where(kept, rank + jnp.where(lane < SEQ, 0.0, 1.0 * CAP), -1.0)
    for item in w_copies:
        item.wait()

    def one_chunk(i, carry):
        slot_iota = lax.broadcasted_iota(jnp.int32, (64, TOK), 0).astype(f32)
        hots, gate_cols = [], []
        rows = pl.ds(pl.multiple_of(i * 256, 256), 256)
        g_parts = []
        for q in range(4):
            m = i * 4 + q
            hot = (slot_iota == slot_s[pl.ds(m, 1), :]).astype(f32)
            gate_col = jnp.sum(hot * gate_s[pl.ds(m, 1), :], axis=1, keepdims=True)
            hot_b = hot.astype(bf16)
            hots.append(hot_b)
            gate_cols.append(gate_col)
            srows = pl.ds(pl.multiple_of(i * 256 + q * 64, 64), 64)
            trows = pl.ds(pl.multiple_of(m * TOK, TOK), TOK)
            disp[srows, :] = dot(hot_b, n2[trows, :]).astype(bf16)
            gsl = dot(hot_b, gx[m, 0:TOK, :])
            g_parts.append(gsl)
            dslot[srows, :] = (gate_col * gsl).astype(bf16)
        gup = dot(disp[rows, :], win[...])
        gate_part, up_part = gup[:, :F], gup[:, F:]
        sig = jax.nn.sigmoid(gate_part)
        hidden = (gate_part * sig * up_part).astype(bf16)
        hid[rows, :] = hidden
        out_rows = dot(hidden, wout[...]).astype(bf16).astype(f32)
        dhid = dot_t(dslot[rows, :], wout[...])
        silu_grad = sig * (1.0 + gate_part * (1.0 - sig))
        dg = jnp.concatenate([dhid * up_part * silu_grad, dhid * gate_part * sig], axis=1).astype(bf16)
        dgu[rows, :] = dg
        din = dot_t(dg, win[...]).astype(bf16)
        for q in range(4):
            part = slice(q * 64, (q + 1) * 64)
            dgate = jnp.sum(g_parts[q] * out_rows[part, :], axis=1, keepdims=True)
            dgate_row = jnp.sum(hots[q].astype(f32) * dgate, axis=0, keepdims=True)
            high = dgate_row.astype(bf16).astype(f32)
            low = dgate_row - high
            line = lax.broadcasted_iota(jnp.int32, (16, TOK), 0)
            extra = jnp.where(line == 2 * c, high, 0.0) + jnp.where(line == 2 * c + 1, low, 0.0)
            obuf[q, 0:TOK, :] = t_dot(hots[q], din[part, :]).astype(bf16)
            obuf[q, TOK:EXT, 0:TOK] = extra.astype(bf16)
            obuf[q, TOK:EXT, TOK:] = jnp.zeros((EXT - TOK, D - TOK), bf16)
            weighted = (gate_cols[q] * out_rows[part, :]).astype(bf16)
            mbuf[q, :, :] = t_dot(hots[q], weighted).astype(bf16)

        @pl.when(i < 2)
        def _():
            c1 = pltpu.make_async_copy(obuf, dn_own.at[pl.ds(i * 4, 4)], o_sem.at[0])
            c2 = pltpu.make_async_copy(mbuf, mix_own.at[pl.ds(i * 4, 4)], o_sem.at[1])
            c1.start()
            c2.start()
            c1.wait()
            c2.wait()

        @pl.when(i >= 2)
        def _():
            c1 = pltpu.make_async_copy(obuf, dn_sib.at[pl.ds(i * 4 - 8, 4)], o_sem.at[0])
            c2 = pltpu.make_async_copy(mbuf, mix_sib.at[pl.ds(i * 4 - 8, 4)], o_sem.at[1])
            c1.start()
            c2.start()
            c1.wait()
            c2.wait()

        return carry

    lax.fori_loop(0, 4, one_chunk, 0)

    def grad_in(b, carry):
        cols = pl.ds(pl.multiple_of(b * 192, 64), 192)
        blk = t_dot(disp[:, cols], dgu[...]) if False else None
        return carry

    for n in range(6):
        wg_rows = slice(n * 256, (n + 1) * 256)
        wg[wg_rows, 0:1024] = t_dot(disp[:, wg_rows], dgu[...]).astype(bf16)
    for n in range(2):
        out_g = t_dot(hid[:, n * 256 : (n + 1) * 256], dslot[...]).astype(bf16)
        for b in range(4):
            blk = n * 4 + b
            for t in range(3):
                wg[blk * 192 + t * 64 : blk * 192 + (t + 1) * 64, 1024:1536] = out_g[
                    b * 64 : (b + 1) * 64, t * 512 : (t + 1) * 512
                ]
    outs = []
    for j in range(4):
        for b in range(2):
            m = j * 2 + b
            blk = (z ^ j) * 2 + (h ^ b)
            outs.append(
                pltpu.make_async_copy(
                    wg.at[pl.ds(pl.multiple_of(blk * 192, 64), 192), :], wg_out[m], g_sem.at[m]
                )
            )
    for item in outs:
        item.start()
    for item in outs:
        item.wait()


def kernel_pair_sum(a_ref, b_ref, *outs):
    for m in range(8):
        outs[m][...] = (a_ref[m].astype(f32) + b_ref[m].astype(f32)).astype(bf16)


def kernel_home(where, gx_ref, resid_ref, n2_ref, gates_ref, misc_ref, *rest):
    pieces = rest[:8]
    dresid_ref, dattn_ref, small_ref, dg_s = rest[8:]
    x, l = where[2], where[4]
    for k in range(4):
        for b in range(2):
            extra = pieces[k * 2 + b][TOK:EXT, 0:TOK].astype(f32)
            first = (l ^ b) * 8 + (x ^ k) * 2
            dg_s[pl.ds(first, 1), :] = extra[0:1, :] + extra[1:2, :]
            dg_s[pl.ds(first + 1, 1), :] = extra[2:3, :] + extra[3:4, :]
    gates = gates_ref[...]
    dgates = dg_s[...]
    dlog = (gates * (dgates - jnp.sum(gates * dgates, axis=0, keepdims=True))).astype(bf16)
    valid_row = jnp.broadcast_to((gx_ref[TOK + 8 : TOK + 9, :TOK].astype(f32) > 0.5).astype(f32), (TOK, TOK))
    valid = valid_row.T[:, 0:1]
    total = t_dot(dlog, misc_ref[0:16, :])
    for piece in pieces:
        total = total + piece[0:TOK, :].astype(f32)
    resid = resid_ref[...]
    rinv = lax.rsqrt(jnp.mean(resid * resid, axis=1, keepdims=True) + EPS)
    u = total * misc_ref[17:18, :].astype(f32)
    g = gx_ref[0:TOK, :].astype(f32) * valid
    dresid = g + rinv * u - resid * (rinv * rinv * rinv) * jnp.mean(u * resid, axis=1, keepdims=True)
    dresid_ref[...] = dresid
    dattn_ref[...] = dresid.astype(bf16)
    small_ref[0:16, :] = dot(dlog, n2_ref[...])
    gain = jnp.sum(total * resid * rinv, axis=0, keepdims=True)
    line = lax.broadcasted_iota(jnp.int32, (16, D), 0)
    small_ref[16:32, :] = jnp.where(line == 1, gain, 0.0)


def kernel_back_o(where, da_own, da_sib, mixed_ref, *rest):
    pieces = rest[:16]
    dmixed_ref = rest[16]
    grads = rest[17:33]
    w, wg, sems, gsems = rest[33:]
    z, x = where[0], where[2]
    copies = o_copies(pieces, w, sems, z, x)
    for item in copies:
        item.start()
    dattn = jnp.concatenate([da_own[...], da_sib[...]], axis=0)
    wg[...] = t_dot(mixed_ref[...], dattn).astype(bf16)
    for item in copies:
        item.wait()
    outs = []
    for j in range(4):
        for k in range(4):
            start = pl.multiple_of(((z ^ j) * 4 + (x ^ k)) * 48, 16)
            outs.append(
                pltpu.make_async_copy(wg.at[pl.ds(start, 48), :], grads[j * 4 + k], gsems.at[j * 4 + k])
            )
    for item in outs:
        item.start()
    dmixed_ref[...] = dot_t(dattn, w[...]).astype(bf16)
    for item in outs:
        item.wait()


def kernel_back(where, xo, xs, dmixed_ref, normed_ref, q_ref, k_ref, v_ref, small_ref, cos_ref, sin_ref, *rest):
    pieces = rest[:16]
    own_ref, sib_ref = rest[16:18]
    grads = rest[18:34]
    w, dq_s, dk_s, dv_s, dcat, wg, sems, gsems = rest[34:]
    z, x = where[0], where[2]
    copies = piece_copies(pieces, w, sems, z, x)
    for item in copies:
        item.start()
    for part, src in enumerate((xo, xs)):
        ok = allowed_mask(src[TOK:EXT, :TOK].astype(f32))
        ok3 = jnp.concatenate([ok.astype(f32)] * 3, axis=0) > 0.5
        rows = slice(part * TOK, (part + 1) * TOK)
        for a in range(4):
            keys = k_ref[rows, a * 64 : (a + 1) * 64]
            vals = v_ref[rows, a * 64 : (a + 1) * 64]
            heads = [slice((3 * a + g) * 64, (3 * a + g + 1) * 64) for g in range(3)]
            q3 = jnp.concatenate([q_ref[rows, hd] for hd in heads], axis=0)
            dm3 = jnp.concatenate([dmixed_ref[rows, hd] for hd in heads], axis=0)
            scores = jnp.where(ok3, dot_t(q3, keys) * 0.125, NEG)
            top = jnp.max(scores, axis=1, keepdims=True)
            expo = jnp.exp(scores - top)
            probs = expo / jnp.sum(expo, axis=1, keepdims=True)
            dprobs = dot_t(dm3, vals)
            dv_s[rows, a * 64 : (a + 1) * 64] = t_dot(probs.astype(bf16), dm3)
            ds = (probs * (dprobs - jnp.sum(probs * dprobs, axis=1, keepdims=True))).astype(bf16)
            dq3 = dot(ds, keys) * 0.125
            for g in range(3):
                dq_s[rows, heads[g]] = dq3[g * TOK : (g + 1) * TOK, :]
            dk_s[rows, a * 64 : (a + 1) * 64] = t_dot(ds, q3) * 0.125
    cos_full, sin_full = cos_ref[...], -sin_ref[...]
    dcat[:, 0:HQ] = turn(dq_s[...], cos_full, sin_full).astype(bf16)
    dcat[:, HQ : HQ + HK] = turn(dk_s[...], cos_full, sin_full).astype(bf16)
    dcat[:, HQ + HK : QKV] = dv_s[...].astype(bf16)
    for item in copies:
        item.wait()
    misc_gain = dot_t(
        (
            lax.broadcasted_iota(jnp.int32, (128, 128), 0)
            == lax.broadcasted_iota(jnp.int32, (128, 128), 1)
        ).astype(f32).astype(bf16),
        w[:, QKV:],
    )[16:17, :]
    del misc_gain
    dnormed = dot_t(dcat[...], w[:, 0:QKV])
    own_ref[...] = dnormed[:TOK, :]
    sib_ref[...] = dnormed[TOK:, :]
    xin = jnp.concatenate([xo[:TOK, :], xs[:TOK, :]], axis=0).astype(f32)
    rinv = lax.rsqrt(jnp.mean(xin * xin, axis=1, keepdims=True) + EPS)
    gain = jnp.sum(dnormed * xin * rinv, axis=0, keepdims=True)
    line = lax.broadcasted_iota(jnp.int32, (32, D), 0)
    small = small_ref[...] + jnp.where(line == 16, gain, 0.0)
    small = jnp.concatenate([small, jnp.zeros((96, D), f32)], axis=0).astype(bf16)
    eye = (
        lax.broadcasted_iota(jnp.int32, (128, 128), 0) == lax.broadcasted_iota(jnp.int32, (128, 128), 1)
    ).astype(f32).astype(bf16)
    wg[:, 0:QKV] = t_dot(normed_ref[...], dcat[...]).astype(bf16)
    wg[:, QKV:] = t_dot(small, eye).astype(bf16)
    outs = []
    for j in range(4):
        for k in range(4):
            for b in range(2):
                start = pl.multiple_of((((z ^ j) * 2 + b) * 4 + (x ^ k)) * 48, 16)
                outs.append(
                    pltpu.make_async_copy(
                        wg.at[pl.ds(start, 48), :],
                        grads[j * 4 + k].at[pl.ds(48 * b, 48), :],
                        gsems.at[(j * 4 + k) * 2 + b],
                    )
                )
    for item in outs:
        item.start()
    for item in outs:
        item.wait()


def kernel_token_grad(xo, dresid_ref, own_ref, recv_ref, misc_ref, out_ref):
    xin = xo[:TOK, :].astype(f32)
    rinv = lax.rsqrt(jnp.mean(xin * xin, axis=1, keepdims=True) + EPS)
    u = (own_ref[...] + recv_ref[...]) * misc_ref[16:17, :].astype(f32)
    out = dresid_ref[...] + rinv * u - xin * (rinv * rinv * rinv) * jnp.mean(u * xin, axis=1, keepdims=True)
    out_ref[...] = out.astype(bf16)


def kernel_block_out(gx_ref, resid_ref, *rest):
    pieces, out_ref = rest[:8], rest[8]
    valid_row = jnp.broadcast_to((gx_ref[TOK + 8 : TOK + 9, :TOK].astype(f32) > 0.5).astype(f32), (TOK, TOK))
    valid = valid_row.T[:, 0:1]
    total = resid_ref[...]
    for piece in pieces:
        total = total + piece[...].astype(f32)
    out_ref[...] = (total * valid).astype(bf16)


def call(body, outs, ins, scratch=(), mib=60, flops=0, nbytes=0, name=None):
    return pl.pallas_call(
        body,
        out_shape=[jax.ShapeDtypeStruct(shape, dtype) for shape, dtype, _ in outs],
        in_specs=[spec for _, spec in ins],
        out_specs=[spec for _, _, spec in outs],
        scratch_shapes=list(scratch),
        compiler_params=params(mib),
        cost_estimate=pl.CostEstimate(flops=flops, bytes_accessed=nbytes, transcendentals=0),
        name=name,
    )(*[value for value, _ in ins])


def sum_pieces(pieces):
    total = pieces[0].astype(f32)
    for piece in pieces[1:]:
        total = total + piece.astype(f32)
    return total


def on_device(
    tokens, segment_ids, routes, cotangent, attn_gain, query_weight, key_weight, value_weight,
    output_weight, expert_gain, router_weight, expert_in, expert_out,
):
    V, A, S = spec_vmem(), spec_any(), spec_smem()
    iz, ih, ix, ic, il = [lax.axis_index(name) for name in AX]
    where = jnp.stack([iz, ih, ix, ic, il]).astype(jnp.int32)
    cos_np, sin_np = rope_tables()
    cos_full, sin_full = jnp.asarray(cos_np), jnp.asarray(sin_np)

    ints = jnp.concatenate(
        [routes.reshape(TOK, TOPK).T, segment_ids.reshape(1, TOK), jnp.zeros((7, TOK), jnp.int32)], axis=0
    ).astype(bf16)
    ints = jnp.pad(ints, ((0, 0), (0, D - TOK)))
    x_own = jnp.concatenate([tokens.reshape(TOK, D), ints], axis=0)
    g_own = jnp.concatenate([cotangent.reshape(TOK, D), ints], axis=0)
    x_sib = send(x_own, dc=1)

    small = jnp.concatenate(
        [router_weight, attn_gain[:, None], expert_gain[:, None], jnp.zeros((12, 110), bf16)], axis=1
    )
    q4 = query_weight.reshape(12, 4, 2, 192)
    k4 = key_weight.reshape(12, 4, 2, 64)
    v4 = value_weight.reshape(12, 4, 2, 64)
    for_core = [
        jnp.concatenate(
            [
                q4[:, :, core].reshape(12, HQ),
                k4[:, :, core].reshape(12, HK),
                v4[:, :, core].reshape(12, HK),
                small,
                output_weight,
            ],
            axis=1,
        )
        for core in range(2)
    ]
    packed = jnp.stack([for_core[0], for_core[0], for_core[1], for_core[1]])
    packed = lax.all_to_all(packed, ("c", "yl"), split_axis=0, concat_axis=0, tiled=True)
    qkv48 = packed[:, :, :QKVM].reshape(48, QKVM)
    o48 = packed[:, :, QKVM:].reshape(48, D)
    qkv_other = send(qkv48, dh=1)
    o_other = send(o48, dh=1)
    qkv96 = jnp.where(
        ih == 0,
        jnp.concatenate([qkv48, qkv_other], axis=0),
        jnp.concatenate([qkv_other, qkv48], axis=0),
    )
    o_mine = jnp.where(ih == ic, o48, o_other)
    pairs = [(j, k) for j in range(4) for k in range(4)]
    qkv_pieces = [qkv96 if (j, k) == (0, 0) else send(qkv96, dz=j, dx=k) for j, k in pairs]
    o_pieces = [o_mine if (j, k) == (0, 0) else send(o_mine, dz=j, dx=k) for j, k in pairs]

    e_in = lax.all_to_all(expert_in, ("x", "c"), split_axis=0, concat_axis=0, tiled=True).reshape(192, 1024)
    e_out = lax.all_to_all(expert_out, ("x", "c"), split_axis=0, concat_axis=0, tiled=True).reshape(64, D)
    e_pack = jnp.concatenate(
        [e_in, jnp.concatenate([e_out[:, t * 512 : (t + 1) * 512] for t in range(3)], axis=0)], axis=1
    )
    e_pairs = [(j, b) for j in range(4) for b in range(2)]
    e_pieces = [e_pack if (j, b) == (0, 0) else send(e_pack, dz=j, dh=b) for j, b in e_pairs]

    p_pairs = [(k, b) for k in range(4) for b in range(2)]

    def spread(value):
        mine = [value if (k, b) == (0, 0) else send(value, dx=k, dl=b) for k, b in p_pairs]
        return mine + [send(item, dc=1) for item in mine]

    gx_pieces = spread(g_own)

    normed, q_b, k_b, v_b, mixed, misc = call(
        kernel_attn,
        [
            ((256, D), bf16, V), ((256, HQ), bf16, V), ((256, HK), bf16, V), ((256, HK), bf16, V),
            ((256, HQ), bf16, V), ((128, D), bf16, V),
        ],
        [(where, S), (x_own, V), (x_sib, V), (cos_full, V), (sin_full, V)] + [(p, A) for p in qkv_pieces],
        [pltpu.VMEM((D, QKVM), bf16), pltpu.SemaphoreType.DMA((32,))],
        flops=2 * 256 * D * QKV, nbytes=8 * 2**20, name="attention",
    )
    part_own, part_sib = call(
        kernel_oproj,
        [((TOK, D), f32, V), ((TOK, D), f32, V)],
        [(where, S), (mixed, V)] + [(p, A) for p in o_pieces],
        [pltpu.VMEM((HQ, D), bf16), pltpu.SemaphoreType.DMA((16,))],
        flops=2 * 256 * D * HQ, nbytes=4 * 2**20, name="output_projection",
    )
    part_recv = send(part_sib, dc=1)
    resid, n2, gates = call(
        kernel_resid,
        [((TOK, D), f32, V), ((TOK, D), bf16, V), ((16, TOK), f32, V)],
        [(x_own, V), (part_own, V), (part_recv, V), (misc, V)],
        flops=10**7, nbytes=3 * 2**20, name="residual_norm",
    )
    n2_pieces = spread(n2)
    outs = call(
        kernel_expert,
        [((8, EXT, D), bf16, A), ((8, EXT, D), bf16, A), ((8, TOK, D), bf16, A), ((8, TOK, D), bf16, A)]
        + [((192, D), bf16, A)] * 8,
        [(where, S), (misc, V)] + [(p, A) for p in n2_pieces + gx_pieces + e_pieces],
        [
            pltpu.VMEM((2048, D), bf16), pltpu.VMEM((16, EXT, D), bf16),
            pltpu.VMEM((D, 1024), bf16), pltpu.VMEM((F, D), bf16),
            pltpu.VMEM((1024, D), bf16), pltpu.VMEM((1024, D), bf16),
            pltpu.VMEM((1024, F), bf16), pltpu.VMEM((1024, 1024), bf16),
            pltpu.VMEM((16, TOK), f32), pltpu.VMEM((16, TOK), f32), pltpu.VMEM((16, TOK), f32),
            pltpu.VMEM((4, EXT, D), bf16), pltpu.VMEM((4, TOK, D), bf16),
            pltpu.VMEM((D, D), bf16),
            pltpu.SemaphoreType.DMA((16,)), pltpu.SemaphoreType.DMA((16,)),
            pltpu.SemaphoreType.DMA((32,)), pltpu.SemaphoreType.DMA((2,)),
            pltpu.SemaphoreType.DMA((8,)),
        ],
        flops=18 * 10**9, nbytes=40 * 2**20, name="experts",
    )
    dn_own, dn_sib, mix_own, mix_sib = outs[:4]
    e_grads = outs[4:]

    def gather_sums(own, sib, rows):
        recv = send(sib, dc=1)
        sums = call(
            kernel_pair_sum, [((rows, D), bf16, V)] * 8, [(own, V), (recv, V)],
            flops=10**7, nbytes=10 * 2**20, name="pair_sum",
        )
        return [sums[i] if (k, b) == (0, 0) else send(sums[i], dx=k, dl=b) for i, (k, b) in enumerate(p_pairs)]

    dn_pieces = gather_sums(dn_own, dn_sib, EXT)
    dresid, dattn, small_grad = call(
        kernel_home,
        [((TOK, D), f32, V), ((TOK, D), bf16, V), ((32, D), f32, V)],
        [(where, S), (g_own, V), (resid, V), (n2, V), (gates, V), (misc, V)] + [(p, V) for p in dn_pieces],
        [pltpu.VMEM((16, TOK), f32)],
        flops=10**8, nbytes=6 * 2**20, name="home_gradient",
    )
    dattn_sib = send(dattn, dc=1)
    outs = call(
        kernel_back_o,
        [((256, HQ), bf16, V)] + [((48, D), bf16, A)] * 16,
        [(where, S), (dattn, V), (dattn_sib, V), (mixed, V)] + [(p, A) for p in o_pieces],
        [
            pltpu.VMEM((HQ, D), bf16), pltpu.VMEM((HQ, D), bf16),
            pltpu.SemaphoreType.DMA((16,)), pltpu.SemaphoreType.DMA((16,)),
        ],
        flops=4 * 256 * D * HQ, nbytes=6 * 2**20, name="output_back",
    )
    dmixed, o_grads = outs[0], outs[1:]
    outs = call(
        kernel_back,
        [((TOK, D), f32, V), ((TOK, D), f32, V)] + [((96, QKVM), bf16, A)] * 16,
        [
            (where, S), (x_own, V), (x_sib, V), (dmixed, V), (normed, V), (q_b, V), (k_b, V), (v_b, V),
            (small_grad, V), (cos_full, V), (sin_full, V),
        ]
        + [(p, A) for p in qkv_pieces],
        [
            pltpu.VMEM((D, QKVM), bf16), pltpu.VMEM((256, HQ), f32), pltpu.VMEM((256, HK), f32),
            pltpu.VMEM((256, HK), f32), pltpu.VMEM((256, QKV), bf16), pltpu.VMEM((D, QKVM), bf16),
            pltpu.SemaphoreType.DMA((32,)), pltpu.SemaphoreType.DMA((32,)),
        ],
        flops=4 * 256 * D * QKV, nbytes=12 * 2**20, name="attention_back",
    )
    dn1_own, dn1_sib, qkv_grads = outs[0], outs[1], outs[2:]
    dn1_recv = send(dn1_sib, dc=1)
    (token_grad,) = call(
        kernel_token_grad, [((TOK, D), bf16, V)],
        [(x_own, V), (dresid, V), (dn1_own, V), (dn1_recv, V), (misc, V)],
        flops=10**7, nbytes=3 * 2**20, name="token_gradient",
    )
    mix_pieces = gather_sums(mix_own, mix_sib, TOK)
    (block_out,) = call(
        kernel_block_out, [((TOK, D), bf16, V)], [(g_own, V), (resid, V)] + [(p, V) for p in mix_pieces],
        flops=10**7, nbytes=5 * 2**20, name="block_output",
    )

    e_sum = sum_pieces(
        [e_grads[0]] + [send(e_grads[i], dz=j, dh=b) for i, (j, b) in enumerate(e_pairs) if i]
    ).astype(bf16)
    ge_in = lax.all_to_all(e_sum[:, :1024].reshape(8, 24, 1024), ("x", "c"), split_axis=0, concat_axis=0, tiled=True)
    ge_out = jnp.concatenate([e_sum[t * 64 : (t + 1) * 64, 1024:] for t in range(3)], axis=1)
    ge_out = lax.all_to_all(ge_out.reshape(8, 8, D), ("x", "c"), split_axis=0, concat_axis=0, tiled=True)

    o_sum = sum_pieces([o_grads[0]] + [send(o_grads[i], dz=j, dx=k) for i, (j, k) in enumerate(pairs) if i])
    o_sum = o_sum.astype(bf16)
    o_swap = send(o_sum, dh=1)
    o_sum = o_sum.astype(f32) + o_swap.astype(f32)
    qkv_sum = sum_pieces([qkv_grads[0]] + [send(qkv_grads[i], dz=j, dx=k) for i, (j, k) in enumerate(pairs) if i])
    keep = jnp.where(ih == 0, qkv_sum[:48], qkv_sum[48:])
    give = jnp.where(ih == 0, qkv_sum[48:], qkv_sum[:48])
    qkv_sum = (keep + send(give.astype(bf16), dh=1).astype(f32)).astype(bf16)
    o_part = jnp.where(ih == ic, o_sum, 0.0).astype(bf16)
    back = jnp.concatenate([qkv_sum, o_part], axis=1).reshape(4, 12, QKVM + D)
    back = lax.all_to_all(back, ("c", "yl"), split_axis=0, concat_axis=0, tiled=True).astype(f32)
    back = back[0::2] + back[1::2]
    dq = jnp.stack([back[core, :, :HQ].reshape(12, 4, 192) for core in range(2)], axis=2).reshape(12, D)
    dk = jnp.stack([back[core, :, HQ : HQ + HK].reshape(12, 4, 64) for core in range(2)], axis=2).reshape(12, 512)
    dv = jnp.stack([back[core, :, HQ + HK : QKV].reshape(12, 4, 64) for core in range(2)], axis=2).reshape(12, 512)
    tail = back[0] + back[1]
    d_o = tail[:, QKVM:]
    d_small = tail[:, QKV:QKVM]
    return (
        block_out.reshape(2, SEQ, D),
        token_grad.reshape(2, SEQ, D),
        d_small[:, 16],
        dq,
        dk,
        dv,
        d_o,
        d_small[:, 17],
        d_small[:, :16],
        ge_in.astype(f32),
        ge_out.astype(f32),
    )


def solution(mesh):
    devices = mesh.devices.reshape(DIMS) if hasattr(mesh, "devices") else None
    fine = Mesh(devices, AX)
    every = ("z", "yh", "x", "c", "yl")
    dp = ("z", "yh", "x", "c")
    in_specs = (
        P(every, None, None), P(every, None), P(every, None, None), P(every, None, None), P(every),
        P(every, None), P(every, None), P(every, None), P(every, None), P(every), P(every, None),
        P("yl", dp, None), P("yl", dp, None),
    )
    out_specs = (
        P(every, None, None), P(every, None, None), P(every), P(every, None), P(every, None),
        P(every, None), P(every, None), P(every), P(every, None), P("yl", dp, None), P("yl", dp, None),
    )
    return jax.shard_map(on_device, mesh=fine, in_specs=in_specs, out_specs=out_specs, check_vma=False)
```

time: 3520 us -> 749 us (0.21)
  blocking collectives: 1350 us -> 0 us
  waiting for transfers between devices: 1070 us -> 293 us
  local copies, waits for them, and re-layouts: 263 us -> 21.1 us
  matrix products: 233 us -> 0 us
  starting transfers between devices: 519 us -> 314 us
  Pallas kernels: 0 us -> 99 us
  other arithmetic: 48.5 us -> 8.7 us
    unnamed x3 -> x0, blocking collectives: 1040 us -> none
    all_gather x6 -> x0, waiting for transfers between devices: 971 us -> none  [the longest x1 306 us: fetch_dense(): lax.all_gather(dense_shards[1], ('dp', 'expert'), axis=0, tiled=True)]
    unnamed x160 -> x0, starting transfers between devices: 487 us -> none
    all_gather x1 -> x0, blocking collectives: 311 us -> none  [fetch_dense(): lax.all_gather(dense_shards[6], ('dp', 'expert'), axis=0, tiled=True)]
    ppermute x0 -> x128, waiting for transfers between devices: none -> 272 us  [send(): return lax.ppermute(value, AX, pairs)]
    ppermute x0 -> x128, starting transfers between devices: none -> 249 us  [send(): return lax.ppermute(value, AX, pairs)]
    dot_general x54 -> x0, matrix products: 233 us -> none  [the longest x2 59.8 us: on_device(): jnp.einsum('secd,secf->edf', received, dgate_up, preferred_element_type=j...]
    unnamed x636 -> x242, local copies, waits for them, and re-layouts: 197 us -> 6.05 us
  transfers between devices with their start and end apart: 176 -> 134, of which waited for: 15 -> 43; matrix products, arithmetic and copies ran while one was open for 38% -> 2% of each run, Pallas kernels for 0% -> 8%
where the time goes in v1:
time: 749 us; the launch traced here: 739 us
  starting transfers between devices  314 us (42%)
  waiting for transfers between devices  293 us (39%)
  Pallas kernels  99 us (13%)
  local copies, waits for them, and re-layouts  21.1 us (3%)
  other arithmetic  8.7 us (1%)
    ppermute x128, waiting for transfers between devices, send(): return lax.ppermute(value, AX, pairs)  272 us
    ppermute x128, starting transfers between devices, send(): return lax.ppermute(value, AX, pairs)  249 us
    pallas_call x11, Pallas kernels, call(): pl.pallas_call(body, out_shape=[jax.ShapeDtypeStruct(shape, dtype) for sh...  99 us
    all_to_all x1, starting transfers between devices, on_device(): lax.all_to_all(ge_out.reshape(8, 8, D), ('x', 'c'), split_axis=0, concat_...  30.9 us
  transfers between devices with their start and end apart: 134, of which 43 were waited for; matrix products, arithmetic and copies ran while one was open for 2% of the time, Pallas kernels for 8%

profile of v1, /device:TPU:1, one launch (start us, length us, event | category | flops | bytes accessed | tf_op | source)
XLA Modules:
  0.0 738.9 jit_solution(7382751941909430275)
XLA Ops:
  18.1 11.0 %all-to-all-done = bf16[4,12,2944]{2,1,0:T(8,128)(2,1)S(1)} async-done(((bf16[4,12,2944]{2,1,0:T(8,128)(2,1)}), bf16[4,12,2944]{2,1,0:T(8,128)(2,1)S(1)}, u32[]{:S(2)}, u32[]{:S(2)}) %all-to-all-start) | async-done | bytes 282656 | tf_op jit(solution)/shard_map/all_to_all | solution.py:581
  95.6 15.9 %collective-permute-start.23 = (bf16[48,1536]{1,0:T(8,128)(2,1)S(1)}, bf16[48,1536]{1,0:T(8,128)(2,1)S(1)}, u32[]{:S(2)}, u32[]{:S(2)}) collective-permute-start(bf16[48,1536]{1,0:T(8,128)(2,1)S(1)} %broadcast_select_fusion.rest_0_), channel_id=1, source_target_pairs={{0,40},{1,41},{2,42},{3,43},{4,44},{5,45},{6,46},{7,47},{8,32},{9,... | collective-permute-start | bytes 442376 | tf_op jit(solution)/shard_map/ppermute | solution.py:46
  124.8 10.1 %collective-permute-done.16.rest_15_ = bf16[96,1408]{1,0:T(8,128)(2,1)S(1)} collective-permute-done((bf16[96,1408]{1,0:T(8,128)(2,1)S(1)}, bf16[96,1408]{1,0:T(8,128)(2,1)S(1)}, u32[]{:S(2)}, u32[]{:S(2)}) %collective-permute-start.16) | collective-permute-done | bytes 270368 | tf_op jit(solution)/shard_map/ppermute | solution.py:46
  140.8 26.2 %collective-permute-done.13.rest_12_ = bf16[96,1408]{1,0:T(8,128)(2,1)S(1)} collective-permute-done((bf16[96,1408]{1,0:T(8,128)(2,1)S(1)}, bf16[96,1408]{1,0:T(8,128)(2,1)S(1)}, u32[]{:S(2)}, u32[]{:S(2)}) %collective-permute-start.13) | collective-permute-done | bytes 270368 | tf_op jit(solution)/shard_map/ppermute | solution.py:46
  174.0 12.0 %collective-permute-done.8.rest_7_ = bf16[96,1408]{1,0:T(8,128)(2,1)S(1)} collective-permute-done((bf16[96,1408]{1,0:T(8,128)(2,1)S(1)}, bf16[96,1408]{1,0:T(8,128)(2,1)S(1)}, u32[]{:S(2)}, u32[]{:S(2)}) %collective-permute-start.8) | collective-permute-done | bytes 270368 | tf_op jit(solution)/shard_map/ppermute | solution.py:46
  195.8 7.6 %all-to-all-done.2 = bf16[8,8,1536]{2,1,0:T(8,128)(2,1)S(1)} async-done(((bf16[8,8,1536]{2,1,0:T(8,128)(2,1)}), bf16[8,8,1536]{2,1,0:T(8,128)(2,1)S(1)}, u32[]{:S(2)}, u32[]{:S(2)}) %all-to-all-start.2) | async-done | bytes 196640 | tf_op jit(solution)/shard_map/all_to_all | solution.py:597
  212.7 8.1 %attention.1 = (bf16[256,1536]{1,0:T(8,128)(2,1)}, bf16[256,768]{1,0:T(8,128)(2,1)}, bf16[256,256]{1,0:T(8,128)(2,1)}, bf16[256,256]{1,0:T(8,128)(2,1)}, bf16[25...) custom-call(s32[5]{0:T(128)} %stack.43.where, bf16[144,1536]{1,0:T(8,128)(2,1)} %copy-done, bf16[144,1536]{1,0:T(8,128)(2,1)} %copy-done.4, ...), custom_call_target="tpu_custom_call" | custom-call | flops 1006632960 | bytes 8388608 | tf_op jit(solution)/shard_map/attention/pallas_call | solution.py:524
  237.6 12.0 %collective-permute-done.70.rest_39_ = bf16[192,1536]{1,0:T(8,128)(2,1)S(1)} collective-permute-done((bf16[192,1536]{1,0:T(8,128)(2,1)S(1)}, bf16[192,1536]{1,0:T(8,128)(2,1)S(1)}, u32[]{:S(2)}, u32[]{:S(2)}) %collective-permute-start.70) | collective-permute-done | bytes 589856 | tf_op jit(solution)/shard_map/ppermute | solution.py:46
  249.7 24.4 %collective-permute-done.69.rest_38_ = bf16[192,1536]{1,0:T(8,128)(2,1)S(1)} collective-permute-done((bf16[192,1536]{1,0:T(8,128)(2,1)S(1)}, bf16[192,1536]{1,0:T(8,128)(2,1)S(1)}, u32[]{:S(2)}, u32[]{:S(2)}) %collective-permute-start.69) | collective-permute-done | bytes 589856 | tf_op jit(solution)/shard_map/ppermute | solution.py:46
  285.8 10.4 %collective-permute-done.65.rest_34_ = bf16[192,1536]{1,0:T(8,128)(2,1)} collective-permute-done((bf16[192,1536]{1,0:T(8,128)(2,1)S(1)}, bf16[192,1536]{1,0:T(8,128)(2,1)}, u32[]{:S(2)}, u32[]{:S(2)}) %collective-permute-start.65) | collective-permute-done | bytes 589856 | tf_op jit(solution)/shard_map/ppermute | solution.py:46
  298.2 11.1 %collective-permute-start.37 = (bf16[128,1536]{1,0:T(8,128)(2,1)}, bf16[128,1536]{1,0:T(8,128)(2,1)S(1)}, u32[]{:S(2)}, u32[]{:S(2)}) collective-permute-start(bf16[128,1536]{1,0:T(8,128)(2,1)} %get-tuple-element.93.rest_0_.n2_ref), channel_id=1, source_target_pairs={{0,8},{1,9},{2,10},{3,11},{4,12},{5,13},{6,14},{7,15},{8,0},{9,1},... | collective-permute-start | bytes 1179656 | tf_op jit(solution)/shard_map/ppermute | solution.py:46
  339.7 40.4 %experts.1 = (bf16[8,144,1536]{2,1,0:T(8,128)(2,1)}, bf16[8,144,1536]{2,1,0:T(8,128)(2,1)}, bf16[8,128,1536]{2,1,0:T(8,128)(2,1)}, bf16[8,128,1536]{2,1,0:T(8,12...) custom-call(s32[5]{0:T(128)} %stack.43.where, ...), custom_call_target="tpu_custom_call" | custom-call | flops 17999998976 | bytes 41943040 | tf_op jit(solution)/shard_map/experts/pallas_call | solution.py:524
  380.9 8.0 %collective-permute-done.79.b_ref = bf16[8,144,1536]{2,1,0:T(8,128)(2,1)S(1)} collective-permute-done((bf16[8,144,1536]{2,1,0:T(8,128)(2,1)}, bf16[8,144,1536]{2,1,0:T(8,128)(2,1)S(1)}, u32[]{:S(2)}, u32[]{:S(2)}) %collective-permute-start.79) | collective-permute-done | bytes 3538976 | tf_op jit(solution)/shard_map/ppermute | solution.py:46
  399.1 8.2 %collective-permute-done.80.rest_1_ = bf16[144,1536]{1,0:T(8,128)(2,1)S(1)} collective-permute-done((bf16[144,1536]{1,0:T(8,128)(2,1)}, bf16[144,1536]{1,0:T(8,128)(2,1)S(1)}, u32[]{:S(2)}, u32[]{:S(2)}) %collective-permute-start.80) | collective-permute-done | bytes 442400 | tf_op jit(solution)/shard_map/ppermute | solution.py:46
  418.7 8.0 %collective-permute-done.83.rest_4_ = bf16[144,1536]{1,0:T(8,128)(2,1)S(1)} collective-permute-done((bf16[144,1536]{1,0:T(8,128)(2,1)}, bf16[144,1536]{1,0:T(8,128)(2,1)S(1)}, u32[]{:S(2)}, u32[]{:S(2)}) %collective-permute-start.83) | collective-permute-done | bytes 442400 | tf_op jit(solution)/shard_map/ppermute | solution.py:46
  465.9 11.5 %collective-permute-done.123 = bf16[192,1536]{1,0:T(8,128)(2,1)S(1)} collective-permute-done((bf16[192,1536]{1,0:T(8,128)(2,1)}, bf16[192,1536]{1,0:T(8,128)(2,1)S(1)}, u32[]{:S(2)}, u32[]{:S(2)}) %collective-permute-start.123) | collective-permute-done | bytes 589856 | tf_op jit(solution)/shard_map/ppermute | solution.py:46
  485.4 30.2 %collective-permute-done.124 = bf16[192,1536]{1,0:T(8,128)(2,1)S(1)} collective-permute-done((bf16[192,1536]{1,0:T(8,128)(2,1)}, bf16[192,1536]{1,0:T(8,128)(2,1)S(1)}, u32[]{:S(2)}, u32[]{:S(2)}) %collective-permute-start.124) | collective-permute-done | bytes 589856 | tf_op jit(solution)/shard_map/ppermute | solution.py:46
  519.2 9.0 %collective-permute-done.126 = bf16[192,1536]{1,0:T(8,128)(2,1)S(1)} collective-permute-done((bf16[192,1536]{1,0:T(8,128)(2,1)}, bf16[192,1536]{1,0:T(8,128)(2,1)S(1)}, u32[]{:S(2)}, u32[]{:S(2)}) %collective-permute-start.126) | collective-permute-done | bytes 589856 | tf_op jit(solution)/shard_map/ppermute | solution.py:46
  538.2 7.7 %collective-permute-start.113 = (bf16[48,1536]{1,0:T(8,128)(2,1)}, bf16[48,1536]{1,0:T(8,128)(2,1)S(1)}, u32[]{:S(2)}, u32[]{:S(2)}) collective-permute-start(bf16[48,1536]{1,0:T(8,128)(2,1)} %get-tuple-element.150), channel_id=1, source_target_pairs={{0,68},{1,69},{2,70},{3,71},{4,64},{5,65},{6,66},{7,67},{8,76},{9,... | collective-permute-start | bytes 442376 | tf_op jit(solution)/shard_map/ppermute | solution.py:46
  560.4 16.3 %attention_back.1 = (f32[128,1536]{1,0:T(8,128)}, f32[128,1536]{1,0:T(8,128)}, bf16[96,1408]{1,0:T(8,128)(2,1)}, bf16[96,1408]{1,0:T(8,128)(2,1)}, bf16[96,1408]...) custom-call(s32[5]{0:T(128)} %stack.43.where, ...), custom_call_target="tpu_custom_call" | custom-call | flops 2013265920 | bytes 12582912 | tf_op jit(solution)/shard_map/attention_back/pallas_call | solution.py:524
  595.6 30.9 %all-to-all-start.5 = ((bf16[8,8,1536]{2,1,0:T(8,128)(2,1)}), bf16[8,8,1536]{2,1,0:T(8,128)(2,1)S(1)}, u32[]{:S(2)}, u32[]{:S(2)}) async-start(bf16[8,8,1536]{2,1,0:T(8,128)(2,1)} %maximum_bitcast_fusion), calls=%async_computation.5 | async-start | bytes 393216 | tf_op jit(solution)/shard_map/all_to_all | solution.py:720
  647.2 19.8 %collective-permute-done.100 = bf16[96,1408]{1,0:T(8,128)(2,1)S(1)} collective-permute-done((bf16[96,1408]{1,0:T(8,128)(2,1)}, bf16[96,1408]{1,0:T(8,128)(2,1)S(1)}, u32[]{:S(2)}, u32[]{:S(2)}) %collective-permute-start.100) | collective-permute-done | bytes 270368 | tf_op jit(solution)/shard_map/ppermute | solution.py:46
  676.7 13.5 %all-to-all-start.4 = ((bf16[8,24,1024]{2,1,0:T(8,128)(2,1)}), bf16[8,24,1024]{2,1,0:T(8,128)(2,1)S(1)}, u32[]{:S(2)}, u32[]{:S(2)}) async-start(bf16[8,24,1024]{2,1,0:T(8,128)(2,1)} %bitcast.17), calls=%async_computation.4 | async-start | bytes 786432 | tf_op jit(solution)/shard_map/all_to_all | solution.py:718
  708.5 8.6 %collective-permute-done.77.rest_6_ = bf16[128,1536]{1,0:T(8,128)(2,1)} collective-permute-done((bf16[128,1536]{1,0:T(8,128)(2,1)}, bf16[128,1536]{1,0:T(8,128)(2,1)}, u32[]{:S(2)}, u32[]{:S(2)}) %collective-permute-start.77) | collective-permute-done | bytes 393248 | tf_op jit(solution)/shard_map/ppermute | solution.py:46
  (569 shorter events, 375.5 us)
Async XLA Ops:
  47.0 38.5 %collective-permute-start.49 = (bf16[144,1536]{1,0:T(8,128)(2,1)S(1)}, bf16[144,1536]{1,0:T(8,128)(2,1)S(1)}, u32[]{:S(2)}, u32[]{:S(2)}) collective-permute-start(bf16[144,1536]{1,0:T(8,128)(2,1)S(1)} %get-tuple-element.186.rest_16_.gx_ref), channel_id=1, source_target_pairs={{0,1},{1,0},{2,3},{3,2},{4,5},{5,4},{6,7},{7,6},{8,9},{9,8},{10,11... | collective-permute-start | bytes 1327112 | tf_op jit(solution)/shard_map/ppermute | solution.py:46
  121.3 45.8 %collective-permute-start.13 = (bf16[96,1408]{1,0:T(8,128)(2,1)S(1)}, bf16[96,1408]{1,0:T(8,128)(2,1)S(1)}, u32[]{:S(2)}, u32[]{:S(2)}) collective-permute-start(bf16[96,1408]{1,0:T(8,128)(2,1)S(1)} %maximum_select_fusion.rest_0_), channel_id=1, source_target_pairs={{0,96},{1,97},{2,98},{3,99},{4,100},{5,101},{6,102},{7,103},{8,104... | collective-permute-start | bytes 811016 | tf_op jit(solution)/shard_map/ppermute | solution.py:46
  123.8 44.1 %collective-permute-start.12 = (bf16[96,1408]{1,0:T(8,128)(2,1)S(1)}, bf16[96,1408]{1,0:T(8,128)(2,1)S(1)}, u32[]{:S(2)}, u32[]{:S(2)}) collective-permute-start(bf16[96,1408]{1,0:T(8,128)(2,1)S(1)} %maximum_select_fusion.rest_0_), channel_id=1, source_target_pairs={{0,76},{1,77},{2,78},{3,79},{4,72},{5,73},{6,74},{7,75},{8,68},{9,... | collective-permute-start | bytes 811016 | tf_op jit(solution)/shard_map/ppermute | solution.py:46
  134.8 36.7 %collective-permute-start.11 = (bf16[96,1408]{1,0:T(8,128)(2,1)S(1)}, bf16[96,1408]{1,0:T(8,128)(2,1)S(1)}, u32[]{:S(2)}, u32[]{:S(2)}) collective-permute-start(bf16[96,1408]{1,0:T(8,128)(2,1)S(1)} %maximum_select_fusion.rest_0_), channel_id=1, source_target_pairs={{0,72},{1,73},{2,74},{3,75},{4,76},{5,77},{6,78},{7,79},{8,64},{9,... | collective-permute-start | bytes 811016 | tf_op jit(solution)/shard_map/ppermute | solution.py:46
  171.6 36.1 %collective-permute-start.5 = (bf16[96,1408]{1,0:T(8,128)(2,1)S(1)}, bf16[96,1408]{1,0:T(8,128)(2,1)}, u32[]{:S(2)}, u32[]{:S(2)}) collective-permute-start(bf16[96,1408]{1,0:T(8,128)(2,1)S(1)} %maximum_select_fusion.rest_0_), channel_id=1, source_target_pairs={{0,32},{1,33},{2,34},{3,35},{4,36},{5,37},{6,38},{7,39},{8,40},{9,... | collective-permute-start | bytes 811016 | tf_op jit(solution)/shard_map/ppermute | solution.py:46
  172.4 38.2 %collective-permute-start.4 = (bf16[96,1408]{1,0:T(8,128)(2,1)S(1)}, bf16[96,1408]{1,0:T(8,128)(2,1)}, u32[]{:S(2)}, u32[]{:S(2)}) collective-permute-start(bf16[96,1408]{1,0:T(8,128)(2,1)S(1)} %maximum_select_fusion.rest_0_), channel_id=1, source_target_pairs={{0,12},{1,13},{2,14},{3,15},{4,8},{5,9},{6,10},{7,11},{8,4},{9,5},... | collective-permute-start | bytes 811016 | tf_op jit(solution)/shard_map/ppermute | solution.py:46
  226.8 48.0 %collective-permute-start.33 = (f32[128,1536]{1,0:T(8,128)}, f32[128,1536]{1,0:T(8,128)S(1)}, u32[]{:S(2)}, u32[]{:S(2)}) collective-permute-start(f32[128,1536]{1,0:T(8,128)} %get-tuple-element.90), channel_id=1, source_target_pairs={{0,2},{1,3},{2,0},{3,1},{4,6},{5,7},{6,4},{7,5},{8,10},{9,11},{10,... | collective-permute-start | bytes 2359304 | tf_op jit(solution)/shard_map/ppermute | solution.py:46
  232.4 41.7 %collective-permute-start.69 = (bf16[192,1536]{1,0:T(8,128)(2,1)S(1)}, bf16[192,1536]{1,0:T(8,128)(2,1)S(1)}, u32[]{:S(2)}, u32[]{:S(2)}) collective-permute-start(bf16[192,1536]{1,0:T(8,128)(2,1)S(1)} %maximum_maximum_fusion.rest_32_), channel_id=1, source_target_pairs={{0,96},{1,97},{2,98},{3,99},{4,100},{5,101},{6,102},{7,103},{8,104... | collective-permute-start | bytes 1769480 | tf_op jit(solution)/shard_map/ppermute | solution.py:46
  234.9 45.8 %collective-permute-start.68 = (bf16[192,1536]{1,0:T(8,128)(2,1)S(1)}, bf16[192,1536]{1,0:T(8,128)(2,1)S(1)}, u32[]{:S(2)}, u32[]{:S(2)}) collective-permute-start(bf16[192,1536]{1,0:T(8,128)(2,1)S(1)} %maximum_maximum_fusion.rest_32_), channel_id=1, source_target_pairs={{0,80},{1,81},{2,82},{3,83},{4,84},{5,85},{6,86},{7,87},{8,88},{9,... | collective-permute-start | bytes 1769480 | tf_op jit(solution)/shard_map/ppermute | solution.py:46
  235.5 48.0 %collective-permute-start.67 = (bf16[192,1536]{1,0:T(8,128)(2,1)S(1)}, bf16[192,1536]{1,0:T(8,128)(2,1)S(1)}, u32[]{:S(2)}, u32[]{:S(2)}) collective-permute-start(bf16[192,1536]{1,0:T(8,128)(2,1)S(1)} %maximum_maximum_fusion.rest_32_), channel_id=1, source_target_pairs={{0,64},{1,65},{2,66},{3,67},{4,68},{5,69},{6,70},{7,71},{8,72},{9,... | collective-permute-start | bytes 1769480 | tf_op jit(solution)/shard_map/ppermute | solution.py:46
  380.6 150.6 %collective-permute-start.71 = (bf16[8,128,1536]{2,1,0:T(8,128)(2,1)}, bf16[8,128,1536]{2,1,0:T(8,128)(2,1)}, u32[]{:S(2)}, u32[]{:S(2)}) collective-permute-start(bf16[8,128,1536]{2,1,0:T(8,128)(2,1)} %get-tuple-element.95), channel_id=1, source_target_pairs={{0,2},{1,3},{2,0},{3,1},{4,6},{5,7},{6,4},{7,5},{8,10},{9,11},{10,... | collective-permute-start | bytes 9437192 | tf_op jit(solution)/shard_map/ppermute | solution.py:46
  462.5 53.1 %collective-permute-start.124 = (bf16[192,1536]{1,0:T(8,128)(2,1)}, bf16[192,1536]{1,0:T(8,128)(2,1)S(1)}, u32[]{:S(2)}, u32[]{:S(2)}) collective-permute-start(bf16[192,1536]{1,0:T(8,128)(2,1)} %get-tuple-element.161), channel_id=1, source_target_pairs={{0,64},{1,65},{2,66},{3,67},{4,68},{5,69},{6,70},{7,71},{8,72},{9,... | collective-permute-start | bytes 1769480 | tf_op jit(solution)/shard_map/ppermute | solution.py:46
  465.3 50.3 %collective-permute-start.125 = (bf16[192,1536]{1,0:T(8,128)(2,1)}, bf16[192,1536]{1,0:T(8,128)(2,1)S(1)}, u32[]{:S(2)}, u32[]{:S(2)}) collective-permute-start(bf16[192,1536]{1,0:T(8,128)(2,1)} %get-tuple-element.162), channel_id=1, source_target_pairs={{0,80},{1,81},{2,82},{3,83},{4,84},{5,85},{6,86},{7,87},{8,88},{9,... | collective-permute-start | bytes 1769480 | tf_op jit(solution)/shard_map/ppermute | solution.py:46
  477.3 50.8 %collective-permute-start.126 = (bf16[192,1536]{1,0:T(8,128)(2,1)}, bf16[192,1536]{1,0:T(8,128)(2,1)S(1)}, u32[]{:S(2)}, u32[]{:S(2)}) collective-permute-start(bf16[192,1536]{1,0:T(8,128)(2,1)} %get-tuple-element.163), channel_id=1, source_target_pairs={{0,96},{1,97},{2,98},{3,99},{4,100},{5,101},{6,102},{7,103},{8,104... | collective-permute-start | bytes 1769480 | tf_op jit(solution)/shard_map/ppermute | solution.py:46
  477.9 52.7 %collective-permute-start.127 = (bf16[192,1536]{1,0:T(8,128)(2,1)}, bf16[192,1536]{1,0:T(8,128)(2,1)}, u32[]{:S(2)}, u32[]{:S(2)}) collective-permute-start(bf16[192,1536]{1,0:T(8,128)(2,1)} %get-tuple-element.164), channel_id=1, source_target_pairs={{0,112},{1,113},{2,114},{3,115},{4,116},{5,117},{6,118},{7,119},{8... | collective-permute-start | bytes 1769480 | tf_op jit(solution)/shard_map/ppermute | solution.py:46
  582.5 48.8 %collective-permute-start.94 = (bf16[96,1408]{1,0:T(8,128)(2,1)}, bf16[96,1408]{1,0:T(8,128)(2,1)S(1)}, u32[]{:S(2)}, u32[]{:S(2)}) collective-permute-start(bf16[96,1408]{1,0:T(8,128)(2,1)} %get-tuple-element.131), channel_id=1, source_target_pairs={{0,40},{1,41},{2,42},{3,43},{4,44},{5,45},{6,46},{7,47},{8,32},{9,... | collective-permute-start | bytes 811016 | tf_op jit(solution)/shard_map/ppermute | solution.py:46
  584.8 51.0 %collective-permute-start.95 = (bf16[96,1408]{1,0:T(8,128)(2,1)}, bf16[96,1408]{1,0:T(8,128)(2,1)S(1)}, u32[]{:S(2)}, u32[]{:S(2)}) collective-permute-start(bf16[96,1408]{1,0:T(8,128)(2,1)} %get-tuple-element.132), channel_id=1, source_target_pairs={{0,44},{1,45},{2,46},{3,47},{4,40},{5,41},{6,42},{7,43},{8,36},{9,... | collective-permute-start | bytes 811016 | tf_op jit(solution)/shard_map/ppermute | solution.py:46
  588.5 48.2 %collective-permute-start.96 = (bf16[96,1408]{1,0:T(8,128)(2,1)}, bf16[96,1408]{1,0:T(8,128)(2,1)S(1)}, u32[]{:S(2)}, u32[]{:S(2)}) collective-permute-start(bf16[96,1408]{1,0:T(8,128)(2,1)} %get-tuple-element.133), channel_id=1, source_target_pairs={{0,64},{1,65},{2,66},{3,67},{4,68},{5,69},{6,70},{7,71},{8,72},{9,... | collective-permute-start | bytes 811016 | tf_op jit(solution)/shard_map/ppermute | solution.py:46
  589.1 49.0 %collective-permute-start.97 = (bf16[96,1408]{1,0:T(8,128)(2,1)}, bf16[96,1408]{1,0:T(8,128)(2,1)S(1)}, u32[]{:S(2)}, u32[]{:S(2)}) collective-permute-start(bf16[96,1408]{1,0:T(8,128)(2,1)} %get-tuple-element.134), channel_id=1, source_target_pairs={{0,68},{1,69},{2,70},{3,71},{4,64},{5,65},{6,66},{7,67},{8,76},{9,... | collective-permute-start | bytes 811016 | tf_op jit(solution)/shard_map/ppermute | solution.py:46
  589.9 50.3 %collective-permute-start.98 = (bf16[96,1408]{1,0:T(8,128)(2,1)}, bf16[96,1408]{1,0:T(8,128)(2,1)S(1)}, u32[]{:S(2)}, u32[]{:S(2)}) collective-permute-start(bf16[96,1408]{1,0:T(8,128)(2,1)} %get-tuple-element.135), channel_id=1, source_target_pairs={{0,72},{1,73},{2,74},{3,75},{4,76},{5,77},{6,78},{7,79},{8,64},{9,... | collective-permute-start | bytes 811016 | tf_op jit(solution)/shard_map/ppermute | solution.py:46
  595.6 81.1 %all-to-all-start.5 = ((bf16[8,8,1536]{2,1,0:T(8,128)(2,1)}), bf16[8,8,1536]{2,1,0:T(8,128)(2,1)S(1)}, u32[]{:S(2)}, u32[]{:S(2)}) async-start(bf16[8,8,1536]{2,1,0:T(8,128)(2,1)} %maximum_bitcast_fusion), calls=%async_computation.5 | async-start | bytes 393216 | tf_op jit(solution)/shard_map/all_to_all | solution.py:720
  646.0 45.3 %collective-permute-start.72 = (bf16[128,1536]{1,0:T(8,128)(2,1)}, bf16[128,1536]{1,0:T(8,128)(2,1)S(1)}, u32[]{:S(2)}, u32[]{:S(2)}) collective-permute-start(bf16[128,1536]{1,0:T(8,128)(2,1)} %get-tuple-element.97), channel_id=1, source_target_pairs={{0,1},{1,0},{2,3},{3,2},{4,5},{5,4},{6,7},{7,6},{8,9},{9,8},{10,11... | collective-permute-start | bytes 1179656 | tf_op jit(solution)/shard_map/ppermute | solution.py:46
  667.1 40.1 %collective-permute-start.74 = (bf16[128,1536]{1,0:T(8,128)(2,1)}, bf16[128,1536]{1,0:T(8,128)(2,1)S(1)}, u32[]{:S(2)}, u32[]{:S(2)}) collective-permute-start(bf16[128,1536]{1,0:T(8,128)(2,1)} %get-tuple-element.99), channel_id=1, source_target_pairs={{0,5},{1,4},{2,7},{3,6},{4,1},{5,0},{6,3},{7,2},{8,13},{9,12},{10,... | collective-permute-start | bytes 1179656 | tf_op jit(solution)/shard_map/ppermute | solution.py:46
  668.9 38.4 %collective-permute-start.75 = (bf16[128,1536]{1,0:T(8,128)(2,1)}, bf16[128,1536]{1,0:T(8,128)(2,1)S(1)}, u32[]{:S(2)}, u32[]{:S(2)}) collective-permute-start(bf16[128,1536]{1,0:T(8,128)(2,1)} %get-tuple-element.100), channel_id=1, source_target_pairs={{0,8},{1,9},{2,10},{3,11},{4,12},{5,13},{6,14},{7,15},{8,0},{9,1},... | collective-permute-start | bytes 1179656 | tf_op jit(solution)/shard_map/ppermute | solution.py:46
  (231 other events, 5486.0 us)

commit v2 on v1

v2 whole, which is shorter than its diff:
```python
import functools

import jax
import jax.numpy as jnp
import numpy as np
from jax import lax
from jax.experimental import pallas as pl
from jax.experimental.pallas import tpu as pltpu
from jax.sharding import Mesh
from jax.sharding import PartitionSpec as P

D = 1536
Q_HEADS = 24
KV_HEADS = 8
HEAD_DIM = 64
F = 512
TOPK = 8
EXPERTS = 16
SEQ = 64
CAP = 32

AX = ("z", "yh", "x", "c", "yl")
DIMS = (4, 2, 4, 2, 2)
EPS = 1e-5
NEG = -1e30
TOK = 128
EXT = 144
HQ = 192
QK = 256
QKV = 320
QKVM = 384
ROWS = 1024
bf16 = jnp.bfloat16
f32 = jnp.float32


def coords_list():
    return list(np.ndindex(*DIMS))


def send(value, dz=0, dh=0, dx=0, dc=0, dl=0):
    flat = {pos: i for i, pos in enumerate(coords_list())}
    pairs = [
        (i, flat[(z ^ dz, h ^ dh, x ^ dx, c ^ dc, l ^ dl)])
        for (z, h, x, c, l), i in flat.items()
    ]
    return lax.ppermute(value, AX, pairs)


def dot(a, b):
    return jnp.dot(a, b, preferred_element_type=f32)


def dot_t(a, b):
    return lax.dot_general(a, b, (((1,), (1,)), ((), ())), preferred_element_type=f32)


def t_dot(a, b):
    return lax.dot_general(a, b, (((0,), (0,)), ((), ())), preferred_element_type=f32)


def params(mib=60):
    return pltpu.CompilerParams(vmem_limit_bytes=mib * 2**20)


def rope_tables():
    angle = np.arange(SEQ)[:, None] * (10000.0 ** (-np.arange(32) * 2.0 / 64))[None, :]
    cosine, sine = np.cos(angle), np.sin(angle)
    cos_full = np.concatenate([cosine, cosine] * 2, axis=1)
    sin_full = np.concatenate([-sine, sine] * 2, axis=1)
    return np.tile(cos_full, (4, 1)).astype(np.float32), np.tile(sin_full, (4, 1)).astype(np.float32)


def turn(values, cos_full, sin_full):
    width = values.shape[1]
    lane = lax.broadcasted_iota(jnp.int32, values.shape, 1)
    ahead = pltpu.roll(values, width - 32, 1)
    behind = pltpu.roll(values, 32, 1)
    partner = jnp.where((lane % 64) < 32, ahead, behind)
    copies = width // 128
    cos_wide = jnp.concatenate([cos_full] * copies, axis=1)
    sin_wide = jnp.concatenate([sin_full] * copies, axis=1)
    return values * cos_wide + partner * sin_wide


def allowed_mask(ints):
    row = jnp.broadcast_to(ints[8:9, :], (TOK, TOK))
    col = row.T
    p = lax.broadcasted_iota(jnp.int32, (TOK, TOK), 0)
    t = lax.broadcasted_iota(jnp.int32, (TOK, TOK), 1)
    return (row == col) & (t <= p) & ((p < SEQ) == (t < SEQ))


def qkv_copies(pieces, target, sems, h, x):
    copies = []
    for k in range(4):
        for b in range(2):
            for zz in range(4):
                start = pl.multiple_of(((zz * 2 + (h ^ b)) * 4 + (x ^ k)) * 48, 16)
                copies.append(
                    pltpu.make_async_copy(
                        pieces[k].at[b, zz], target.at[pl.ds(start, 48), :], sems.at[(k * 2 + b) * 4 + zz]
                    )
                )
    return copies


def o_copies(pieces, target, sems, x):
    return [
        pltpu.make_async_copy(
            pieces[k], target.at[pl.ds(pl.multiple_of((x ^ k) * 48, 16), 48), :], sems.at[k]
        )
        for k in range(4)
    ]


def spec_any():
    return pl.BlockSpec(memory_space=pl.ANY)


def spec_vmem():
    return pl.BlockSpec(memory_space=pltpu.VMEM)


def spec_smem():
    return pl.BlockSpec(memory_space=pltpu.SMEM)


def unit(size):
    row = lax.broadcasted_iota(jnp.int32, (size, size), 0)
    return (row == lax.broadcasted_iota(jnp.int32, (size, size), 1)).astype(f32).astype(bf16)


def kernel_attn(where, cos_ref, sin_ref, *rest):
    x_in, w_in, wo_in = rest[:8], rest[8:12], rest[12:16]
    normed_ref, qk_ref, v_ref, mixed_ref, misc_ref, own_ref, sib_ref = rest[16:23]
    w, wo, sems, osems = rest[23:]
    copies = qkv_copies(w_in, w, sems, where[1], where[2])
    more = o_copies(wo_in, wo, osems, where[2])
    for item in copies + more:
        item.start()
    for item in copies:
        item.wait()
    misc = dot_t(unit(64), w[:, QKV:])
    misc_ref[...] = misc.astype(bf16)
    gain = misc[16:17, :]
    for m in range(8):
        rows = slice(m * TOK, (m + 1) * TOK)
        xin = x_in[m][0:TOK, :].astype(f32)
        rinv = lax.rsqrt(jnp.mean(xin * xin, axis=1, keepdims=True) + EPS)
        normed_ref[rows, :] = (xin * rinv * gain).astype(bf16)
    cos_full, sin_full = cos_ref[...], sin_ref[...]
    for m in range(4):
        rows = slice(m * 256, (m + 1) * 256)
        qkv = dot(normed_ref[rows, :], w[:, 0:QKVM])
        qk_ref[rows, :] = turn(qkv[:, 0:QK], cos_full, sin_full).astype(bf16)
        v_ref[rows, :] = qkv[:, QK:QKVM].astype(bf16)
    for m in range(8):
        ok = allowed_mask(x_in[m][TOK:EXT, :TOK].astype(f32))
        ok3 = jnp.concatenate([ok.astype(f32)] * 3, axis=0) > 0.5
        rows = slice(m * TOK, (m + 1) * TOK)
        keys = qk_ref[rows, HQ:QK]
        vals = v_ref[rows, 0:64]
        q3 = jnp.concatenate([qk_ref[rows, g * 64 : (g + 1) * 64] for g in range(3)], axis=0)
        scores = jnp.where(ok3, dot_t(q3, keys) * 0.125, NEG)
        top = jnp.max(scores, axis=1, keepdims=True)
        expo = jnp.exp(scores - top)
        probs = (expo / jnp.sum(expo, axis=1, keepdims=True)).astype(bf16)
        out = dot(probs, vals).astype(bf16)
        for g in range(3):
            mixed_ref[rows, g * 64 : (g + 1) * 64] = out[g * TOK : (g + 1) * TOK, :]
    for item in more:
        item.wait()
    for m in range(4):
        rows = slice(m * TOK, (m + 1) * TOK)
        own_ref[m] = dot(mixed_ref[rows, :], wo[...])
        rows = slice((4 + m) * TOK, (5 + m) * TOK)
        sib_ref[m] = dot(mixed_ref[rows, :], wo[...]).astype(bf16)


def kernel_core_sum(own_ref, recv_ref, *outs):
    for m in range(4):
        outs[m][...] = (own_ref[m] + recv_ref[m].astype(f32)).astype(bf16)


def chosen_gates(misc, n2, ints):
    logits = dot_t(misc, n2)
    expert = lax.broadcasted_iota(jnp.int32, logits.shape, 0).astype(f32)
    hot = jnp.zeros(logits.shape, f32)
    for k in range(TOPK):
        hot = jnp.maximum(hot, (expert == ints[k : k + 1, :]).astype(f32))
    masked = jnp.where(hot > 0.5, logits, NEG)
    expo = jnp.where(hot > 0.5, jnp.exp(masked - jnp.max(masked, axis=0, keepdims=True)), 0.0)
    return expo / jnp.sum(expo, axis=0, keepdims=True)


def kernel_resid(xo, p0, p1, p2, p3, misc_ref, resid_ref, n2_ref, gates_ref, na_ref, nb_ref):
    resid = xo[:TOK, :].astype(f32)
    for piece in (p0, p1, p2, p3):
        resid = resid + piece[...].astype(f32)
    resid_ref[...] = resid
    rinv = lax.rsqrt(jnp.mean(resid * resid, axis=1, keepdims=True) + EPS)
    n2 = (resid * rinv * misc_ref[17:18, :].astype(f32)).astype(bf16)
    n2_ref[...] = n2
    for m in range(8):
        na_ref[m] = n2[:SEQ, :]
        nb_ref[m] = n2[SEQ:, :]
    gates_ref[...] = chosen_gates(misc_ref[0:16, :], n2, xo[TOK:EXT, :TOK].astype(f32))


def kernel_expert(half, where, misc_ref, n2_own, n2_sib, w_ref, *rest):
    gx_in = rest[:4]
    dn_own, mix_own, disp, dslot, hid, dgu = rest[4:10]
    dn_sib, mix_sib = rest[10:14], rest[14:18]
    n2, gx, win, wout, slot_s, gate_s, ints_s, n2_sem, gx_sem, w_sem = rest[18:]
    x, c, l = where[2], where[3], where[4]
    me = (l * 8 + x * 2 + c).astype(f32)
    w_copies = []
    for blk in range(8):
        w_copies.append(
            pltpu.make_async_copy(
                w_ref.at[pl.ds(blk * 192, 192), pl.ds(0, 1024)], win.at[pl.ds(blk * 192, 192), :], w_sem.at[blk * 4]
            )
        )
        for t in range(3):
            w_copies.append(
                pltpu.make_async_copy(
                    w_ref.at[pl.ds(blk * 192 + 64 * t, 64), pl.ds(1024, 512)],
                    wout.at[pl.ds(blk * 64, 64), pl.ds(512 * t, 512)],
                    w_sem.at[blk * 4 + 1 + t],
                )
            )
    n2_copies = [
        pltpu.make_async_copy(n2_own, n2.at[pl.ds(0, 8)], n2_sem.at[0]),
        pltpu.make_async_copy(n2_sib, n2.at[pl.ds(8, 8)], n2_sem.at[1]),
    ]
    gx_copies = []
    for core in range(2):
        for k in range(4):
            for b in range(2):
                at = core * 8 + (x ^ k) * 2 + (l ^ b)
                g_src = gx_in[core * 2 + b].at[k]
                gx_copies.append(
                    pltpu.make_async_copy(
                        g_src.at[pl.ds(SEQ * half, SEQ), :], gx.at[at, pl.ds(0, SEQ), :], gx_sem.at[(core * 8 + k * 2 + b) * 2]
                    )
                )
                gx_copies.append(
                    pltpu.make_async_copy(
                        g_src.at[pl.ds(TOK, 16), :], gx.at[at, pl.ds(SEQ, 16), :], gx_sem.at[(core * 8 + k * 2 + b) * 2 + 1]
                    )
                )
    for item in gx_copies + n2_copies + w_copies:
        item.start()
    for item in gx_copies + n2_copies:
        item.wait()
    for m in range(16):
        ints_s[:, SEQ * m : SEQ * (m + 1)] = gx[m, SEQ : SEQ + 16, SEQ * half : SEQ * (half + 1)].astype(f32)
    token = lax.broadcasted_iota(jnp.int32, (TOK, TOK), 0)
    after = lax.broadcasted_iota(jnp.int32, (TOK, TOK), 1)
    before = ((token < after) & ((token < SEQ) == (after < SEQ))).astype(f32).astype(bf16)
    for core in range(2):
        lanes = slice(core * 512, core * 512 + 512)
        ints = ints_s[:, lanes]
        gates = chosen_gates(misc_ref[0:16, :], n2[8 * core : 8 * core + 8].reshape(512, D), ints)
        expert = lax.broadcasted_iota(jnp.int32, gates.shape, 0).astype(f32)
        gate = jnp.sum(jnp.where(expert == me, gates, 0.0), axis=0, keepdims=True)
        hit = jnp.max((ints[0:8, :] == me).astype(f32), axis=0, keepdims=True)
        hit = hit * (ints[8:9, :] > 0.5).astype(f32)
        rank = jnp.concatenate(
            [
                dot(jnp.broadcast_to(hit[:, u * TOK : (u + 1) * TOK], (16, TOK)).astype(bf16), before)[0:1, :]
                for u in range(4)
            ],
            axis=1,
        )
        slot = jnp.where((hit > 0.5) & (rank < CAP - 0.5), rank, -1.0)
        for q in range(8):
            slot_s[core * 8 + q : core * 8 + q + 1, :] = slot[:, q * SEQ : (q + 1) * SEQ]
            gate_s[core * 8 + q : core * 8 + q + 1, :] = gate[:, q * SEQ : (q + 1) * SEQ]
    for item in w_copies:
        item.wait()

    def one_chunk(i, carry):
        rows = pl.ds(pl.multiple_of(i * 256, 256), 256)
        slot_iota = lax.broadcasted_iota(jnp.int32, (CAP, SEQ), 0).astype(f32)
        hots, gate_cols, g_parts = [], [], []
        for q in range(8):
            m = i * 8 + q
            hot = (slot_iota == slot_s[pl.ds(m, 1), :]).astype(f32)
            gate_col = jnp.sum(hot * gate_s[pl.ds(m, 1), :], axis=1, keepdims=True)
            hot_b = hot.astype(bf16)
            hots.append(hot_b)
            gate_cols.append(gate_col)
            srows = pl.ds(pl.multiple_of(i * 256 + q * CAP, CAP), CAP)
            disp[srows, :] = dot(hot_b, n2[m]).astype(bf16)
            gsl = dot(hot_b, gx[m, 0:SEQ, :])
            g_parts.append(gsl)
            dslot[srows, :] = (gate_col * gsl).astype(bf16)
        gup = dot(disp[rows, :], win[...])
        gate_part, up_part = gup[:, :F], gup[:, F:]
        sig = jax.nn.sigmoid(gate_part)
        hidden = (gate_part * sig * up_part).astype(bf16)
        hid[rows, :] = hidden
        out_rows = dot(hidden, wout[...]).astype(bf16).astype(f32)
        dhid = dot_t(dslot[rows, :], wout[...])
        silu_grad = sig * (1.0 + gate_part * (1.0 - sig))
        dg = jnp.concatenate([dhid * up_part * silu_grad, dhid * gate_part * sig], axis=1).astype(bf16)
        dgu[rows, :] = dg
        din = dot_t(dg, win[...]).astype(bf16)

        def give(dn_refs, mix_refs):
            for q in range(8):
                dn_ref, mix_ref = dn_refs[q], mix_refs[q]
                part = slice(q * CAP, (q + 1) * CAP)
                dgate = jnp.sum(g_parts[q] * out_rows[part, :], axis=1, keepdims=True)
                dgate_row = jnp.sum(hots[q].astype(f32) * dgate, axis=0, keepdims=True)
                high = dgate_row.astype(bf16).astype(f32)
                low = dgate_row - high
                line = lax.broadcasted_iota(jnp.int32, (16, SEQ), 0)
                extra = jnp.where(line == 2 * c, high, 0.0) + jnp.where(line == 2 * c + 1, low, 0.0)
                dn_ref[0:SEQ, :] = t_dot(hots[q], din[part, :]).astype(bf16)
                dn_ref[SEQ : SEQ + 16, :] = jnp.zeros((16, D), bf16)
                dn_ref[SEQ : SEQ + 16, 0:SEQ] = extra.astype(bf16)
                weighted = (gate_cols[q] * out_rows[part, :]).astype(bf16)
                mix_ref[...] = t_dot(hots[q], weighted).astype(bf16)

        @pl.when(i == 0)
        def _():
            give([dn_own.at[q] for q in range(8)], [mix_own.at[q] for q in range(8)])

        @pl.when(i == 1)
        def _():
            give([dn_sib[q // 2].at[q % 2] for q in range(8)], [mix_sib[q // 2].at[q % 2] for q in range(8)])

        return carry

    lax.fori_loop(0, 2, one_chunk, 0)


def kernel_expert_grads(disp_a, dslot_a, hid_a, dgu_a, disp_b, dslot_b, hid_b, dgu_b, wg):
    for n in range(6):
        cols = slice(n * 256, (n + 1) * 256)
        wg[cols, 0:1024] = (t_dot(disp_a[:, cols], dgu_a[...]) + t_dot(disp_b[:, cols], dgu_b[...])).astype(bf16)
    for n in range(2):
        cols = slice(n * 256, (n + 1) * 256)
        out_g = (t_dot(hid_a[:, cols], dslot_a[...]) + t_dot(hid_b[:, cols], dslot_b[...])).astype(bf16)
        for b in range(4):
            blk = n * 4 + b
            for t in range(3):
                wg[blk * 192 + t * 64 : blk * 192 + (t + 1) * 64, 1024:1536] = out_g[
                    b * 64 : (b + 1) * 64, t * 512 : (t + 1) * 512
                ]


def kernel_pair_sum(*refs):
    out = refs[-1]
    lines = 0
    for i in range(0, len(refs) - 1, 5):
        size = refs[i].shape[1]
        for m in range(8):
            total = refs[i][m].astype(f32) + refs[i + 1 + m // 2][m % 2].astype(f32)
            out[m, lines : lines + size, :] = total.astype(bf16)
        lines += size


def kernel_mix_sum(where, *refs):
    l = where[4]
    for out, line in ((refs[10], l), (refs[11], 1 - l)):
        for xx in range(4):
            for half in range(2):
                own, sib = refs[5 * half], refs[5 * half + 1 + xx]
                total = own[xx * 2 + line].astype(f32) + sib[line].astype(f32)
                out[xx, SEQ * half : SEQ * (half + 1), :] = total.astype(bf16)


def kernel_mix_pair(where, keep_ref, recv_ref, *outs):
    for k in range(4):
        xx = where[2] ^ k
        outs[k][...] = (keep_ref[xx].astype(f32) + recv_ref[xx].astype(f32)).astype(bf16)


def kernel_home(gx_ref, resid_ref, n2_ref, gates_ref, misc_ref, dn_a, dn_b, dresid_ref, dattn_ref, small_ref, dg_s):
    for xx in range(4):
        for ll in range(2):
            for half, dn in enumerate((dn_a, dn_b)):
                extra = dn[xx * 2 + ll, SEQ : SEQ + 16, 0:SEQ].astype(f32)
                first = ll * 8 + xx * 2
                lanes = slice(SEQ * half, SEQ * (half + 1))
                dg_s[first : first + 1, lanes] = extra[0:1, :] + extra[1:2, :]
                dg_s[first + 1 : first + 2, lanes] = extra[2:3, :] + extra[3:4, :]
    gates = gates_ref[...]
    dgates = dg_s[...]
    dlog = (gates * (dgates - jnp.sum(gates * dgates, axis=0, keepdims=True))).astype(bf16)
    valid_row = jnp.broadcast_to((gx_ref[TOK + 8 : TOK + 9, :TOK].astype(f32) > 0.5).astype(f32), (TOK, TOK))
    valid = valid_row.T[:, 0:1]
    total = t_dot(dlog, misc_ref[0:16, :])
    sums = []
    for dn in (dn_a, dn_b):
        part = dn[0, 0:SEQ, :].astype(f32)
        for m in range(1, 8):
            part = part + dn[m, 0:SEQ, :].astype(f32)
        sums.append(part)
    total = total + jnp.concatenate(sums, axis=0)
    resid = resid_ref[...]
    rinv = lax.rsqrt(jnp.mean(resid * resid, axis=1, keepdims=True) + EPS)
    u = total * misc_ref[17:18, :].astype(f32)
    g = gx_ref[0:TOK, :].astype(f32) * valid
    dresid = g + rinv * u - resid * (rinv * rinv * rinv) * jnp.mean(u * resid, axis=1, keepdims=True)
    dresid_ref[...] = dresid
    dattn_ref[...] = dresid.astype(bf16)
    small_ref[0:16, :] = dot(dlog, n2_ref[...])
    gain = jnp.sum(total * resid * rinv, axis=0, keepdims=True)
    line = lax.broadcasted_iota(jnp.int32, (16, D), 0)
    small_ref[16:32, :] = jnp.where(line == 1, gain, 0.0)


def kernel_back(where, normed_ref, qk_ref, v_ref, mixed_ref, small_ref, cos_ref, sin_ref, *rest):
    x_in, da_in, w_in, wo_in = rest[:8], rest[8:16], rest[16:20], rest[20:24]
    own_ref, sib_ref = rest[24:26]
    w_out, o_out = rest[26:30], rest[30:34]
    w, wo, da, dmixed, dqk, dcat, wg, og, sems, osems, gsems = rest[34:]
    h, x = where[1], where[2]
    o_in = o_copies(wo_in, wo, osems, x)
    copies = qkv_copies(w_in, w, sems, h, x)
    for item in o_in + copies:
        item.start()
    for m in range(8):
        da[m * TOK : (m + 1) * TOK, :] = da_in[m][...]
    for item in o_in:
        item.wait()
    for m in range(4):
        rows = slice(m * 256, (m + 1) * 256)
        dmixed[rows, :] = dot_t(da[rows, :], wo[...]).astype(bf16)
    for m in range(8):
        ok = allowed_mask(x_in[m][TOK:EXT, :TOK].astype(f32))
        ok3 = jnp.concatenate([ok.astype(f32)] * 3, axis=0) > 0.5
        rows = slice(m * TOK, (m + 1) * TOK)
        keys = qk_ref[rows, HQ:QK]
        vals = v_ref[rows, 0:64]
        q3 = jnp.concatenate([qk_ref[rows, g * 64 : (g + 1) * 64] for g in range(3)], axis=0)
        dm3 = jnp.concatenate([dmixed[rows, g * 64 : (g + 1) * 64] for g in range(3)], axis=0)
        scores = jnp.where(ok3, dot_t(q3, keys) * 0.125, NEG)
        top = jnp.max(scores, axis=1, keepdims=True)
        expo = jnp.exp(scores - top)
        probs = expo / jnp.sum(expo, axis=1, keepdims=True)
        dprobs = dot_t(dm3, vals)
        dcat[rows, QK:QKV] = t_dot(probs.astype(bf16), dm3).astype(bf16)
        ds = (probs * (dprobs - jnp.sum(probs * dprobs, axis=1, keepdims=True))).astype(bf16)
        dq3 = dot(ds, keys) * 0.125
        for g in range(3):
            dqk[rows, g * 64 : (g + 1) * 64] = dq3[g * TOK : (g + 1) * TOK, :]
        dqk[rows, HQ:QK] = t_dot(ds, q3) * 0.125
    cos_full, sin_full = cos_ref[...], -sin_ref[...]
    for m in range(4):
        rows = slice(m * 256, (m + 1) * 256)
        dcat[rows, 0:QK] = turn(dqk[rows, :], cos_full, sin_full).astype(bf16)
    dcat[:, QKV:] = jnp.zeros((ROWS, QKVM - QKV), bf16)
    for item in copies:
        item.wait()
    w[:, QKV:] = jnp.zeros((D, QKVM - QKV), bf16)
    gain = jnp.zeros((1, D), f32)
    for m in range(8):
        rows = slice(m * TOK, (m + 1) * TOK)
        dnormed = dot_t(dcat[rows, :], w[...])
        xin = x_in[m][0:TOK, :].astype(f32)
        rinv = lax.rsqrt(jnp.mean(xin * xin, axis=1, keepdims=True) + EPS)
        gain = gain + jnp.sum(dnormed * xin * rinv, axis=0, keepdims=True)
        if m < 4:
            own_ref[m] = dnormed
        else:
            sib_ref[m - 4] = dnormed.astype(bf16)
    line = lax.broadcasted_iota(jnp.int32, (32, D), 0)
    small = small_ref[...] + jnp.where(line == 16, gain, 0.0)
    small = jnp.concatenate([small, jnp.zeros((32, D), f32)], axis=0).astype(bf16)
    og[...] = t_dot(mixed_ref[...], da[...]).astype(bf16)
    wg[:, 0:QKVM] = t_dot(normed_ref[...], dcat[...]).astype(bf16)
    wg[:, QKV:] = t_dot(small, unit(64)).astype(bf16)
    outs = []
    for k in range(4):
        for b in range(2):
            for zz in range(4):
                start = pl.multiple_of(((zz * 2 + (h ^ b)) * 4 + (x ^ k)) * 48, 16)
                outs.append(
                    pltpu.make_async_copy(
                        wg.at[pl.ds(start, 48), :], w_out[k].at[b, zz], gsems.at[(k * 2 + b) * 4 + zz]
                    )
                )
        start = pl.multiple_of((x ^ k) * 48, 16)
        outs.append(pltpu.make_async_copy(og.at[pl.ds(start, 48), :], o_out[k], gsems.at[32 + k]))
    for item in outs:
        item.start()
    for item in outs:
        item.wait()


def kernel_dense_sum(where, *refs):
    w_in, o_in = refs[:4], refs[4:8]
    w_keep, w_give, o_keep, o_give = refs[8:]
    for b, out in enumerate((w_keep, w_give)):
        for zz in range(4):
            total = w_in[0][b, zz].astype(f32)
            for k in range(1, 4):
                total = total + w_in[k][b, zz].astype(f32)
            out[zz] = total.astype(bf16)
    total = o_in[0][...].astype(f32)
    for k in range(1, 4):
        total = total + o_in[k][...].astype(f32)
    here = where[1] == where[3]
    o_keep[...] = jnp.where(here, total, 0.0).astype(bf16)
    o_give[...] = jnp.where(here, 0.0, total).astype(bf16)


def kernel_token_grad(xo, dresid_ref, p0, p1, p2, p3, misc_ref, out_ref):
    xin = xo[:TOK, :].astype(f32)
    rinv = lax.rsqrt(jnp.mean(xin * xin, axis=1, keepdims=True) + EPS)
    u = p0[...].astype(f32)
    for piece in (p1, p2, p3):
        u = u + piece[...].astype(f32)
    u = u * misc_ref[16:17, :].astype(f32)
    out = dresid_ref[...] + rinv * u - xin * (rinv * rinv * rinv) * jnp.mean(u * xin, axis=1, keepdims=True)
    out_ref[...] = out.astype(bf16)


def kernel_block_out(gx_ref, resid_ref, *rest):
    pieces, out_ref = rest[:4], rest[4]
    valid_row = jnp.broadcast_to((gx_ref[TOK + 8 : TOK + 9, :TOK].astype(f32) > 0.5).astype(f32), (TOK, TOK))
    valid = valid_row.T[:, 0:1]
    total = resid_ref[...]
    for piece in pieces:
        total = total + piece[...].astype(f32)
    out_ref[...] = (total * valid).astype(bf16)


def call(body, outs, ins, scratch=(), mib=60, flops=0, nbytes=0, name=None):
    return pl.pallas_call(
        body,
        out_shape=[jax.ShapeDtypeStruct(shape, dtype) for shape, dtype, _ in outs],
        in_specs=[spec for _, spec in ins],
        out_specs=[spec for _, _, spec in outs],
        scratch_shapes=list(scratch),
        compiler_params=params(mib),
        cost_estimate=pl.CostEstimate(flops=flops // 10**4, bytes_accessed=nbytes // 10**4, transcendentals=0),
        name=name,
    )(*[value for value, _ in ins])


def sum_pieces(pieces):
    total = pieces[0].astype(f32)
    for piece in pieces[1:]:
        total = total + piece.astype(f32)
    return total


def all_gather_z(value):
    spread = jnp.broadcast_to(value[None], (4,) + value.shape)
    return lax.all_to_all(spread, "z", split_axis=0, concat_axis=0, tiled=True)


def pick(value, axis, index):
    return lax.dynamic_index_in_dim(value, index, axis, keepdims=False)


def on_device(
    tokens, segment_ids, routes, cotangent, attn_gain, query_weight, key_weight, value_weight,
    output_weight, expert_gain, router_weight, expert_in, expert_out,
):
    V, A, S = spec_vmem(), spec_any(), spec_smem()
    iz, ih, ix, ic, il = [lax.axis_index(name) for name in AX]
    where = jnp.stack([iz, ih, ix, ic, il]).astype(jnp.int32)
    cos_np, sin_np = rope_tables()
    cos_full, sin_full = jnp.asarray(cos_np), jnp.asarray(sin_np)

    ints = jnp.concatenate(
        [routes.reshape(TOK, TOPK).T, segment_ids.reshape(1, TOK), jnp.zeros((7, TOK), jnp.int32)], axis=0
    ).astype(bf16)
    ints = jnp.pad(ints, ((0, 0), (0, D - TOK)))
    x_own = jnp.concatenate([tokens.reshape(TOK, D), ints], axis=0)
    g_own = jnp.concatenate([cotangent.reshape(TOK, D), ints], axis=0)
    small = jnp.concatenate(
        [router_weight, attn_gain[:, None], expert_gain[:, None], jnp.zeros((12, 46), bf16)], axis=1
    )
    heads = jnp.concatenate(
        [
            query_weight.reshape(12, 8, 192),
            key_weight.reshape(12, 8, 64),
            value_weight.reshape(12, 8, 64),
            jnp.broadcast_to(small[:, None, :], (12, 8, 64)),
        ],
        axis=2,
    ).transpose(1, 0, 2)
    heads = jnp.broadcast_to(heads[:, None], (8, 2, 12, QKVM)).reshape(16, 12, QKVM)
    heads = lax.all_to_all(heads, ("z", "c", "yl"), split_axis=0, concat_axis=0, tiled=True)
    heads = heads.reshape(4, 48, QKVM)
    o_in = jnp.stack(
        [output_weight, send(output_weight, dl=1), send(output_weight, dc=1), send(output_weight, dc=1, dl=1)]
    )
    o48 = jnp.take(o_in, (ic * 2 + il) ^ jnp.arange(4), axis=0, mode="clip").reshape(48, D)
    expert_in, heads = lax.optimization_barrier((expert_in, heads))
    heads = jnp.stack([heads, send(heads, dh=1, dl=1)])
    x_z = [x_own] + [send(x_own, dz=j) for j in (1, 2, 3)]
    o48, heads, x_z = lax.optimization_barrier((o48, heads, x_z))
    o48 = jnp.where(ih == ic, o48, send(o48, dh=1, dl=1))
    w_pieces = [heads] + [send(heads, dx=k) for k in (1, 2, 3)]
    o_pieces = [o48] + [send(o48, dx=k) for k in (1, 2, 3)]
    dense = [(p, A) for p in w_pieces + o_pieces]

    x_all = x_z + [send(item, dc=1) for item in x_z]

    g_x = jnp.stack([g_own] + [send(g_own, dx=k) for k in (1, 2, 3)])
    g_xy = [g_x, send(g_x, dl=1)]

    e_out = expert_out.reshape(8, 8, 3, 512).transpose(0, 2, 1, 3).reshape(8, 24, 512)
    e_pack = jnp.concatenate([expert_in, e_out], axis=2)
    e_pack = lax.all_to_all(e_pack, ("x", "c"), split_axis=0, concat_axis=0, tiled=True)
    e_out = e_pack[:, :, 1024:].reshape(8, 3, 8, 512).transpose(1, 0, 2, 3).reshape(192, 512)
    e_pack = jnp.concatenate([e_pack[:, :, :1024].reshape(192, 1024), e_out], axis=1)
    e_full = lax.all_gather(e_pack, ("z", "yh"), axis=0, tiled=True)

    normed, qk_b, v_b, mixed, misc, part_own, part_sib = call(
        kernel_attn,
        [
            ((ROWS, D), bf16, V), ((ROWS, QK), bf16, V), ((ROWS, 128), bf16, V), ((ROWS, HQ), bf16, V),
            ((64, D), bf16, V), ((4, TOK, D), f32, V), ((4, TOK, D), bf16, V),
        ],
        [(where, S), (cos_full, V), (sin_full, V)] + [(p, V) for p in x_all] + dense,
        [
            pltpu.VMEM((D, QKVM), bf16), pltpu.VMEM((HQ, D), bf16),
            pltpu.SemaphoreType.DMA((32,)), pltpu.SemaphoreType.DMA((4,)),
        ],
        flops=2 * ROWS * D * 512, nbytes=12 * 2**20, name="attention",
    )

    def core_sum(own, sib):
        return call(
            kernel_core_sum, [((TOK, D), bf16, V)] * 4, [(own, V), (send(sib, dc=1), V)],
            flops=10**6, nbytes=6 * 2**20, name="core_sum",
        )

    def team_sum(parts):
        return [parts[0]] + [send(parts[j], dz=j) for j in (1, 2, 3)]

    g_all = g_xy + [send(item, dc=1) for item in g_xy]
    attn_pieces = team_sum(core_sum(part_own, part_sib))
    attn_pieces, g_all = lax.optimization_barrier((attn_pieces, g_all))
    resid, n2, gates, n2_a, n2_b = call(
        kernel_resid,
        [
            ((TOK, D), f32, V), ((TOK, D), bf16, V), ((16, TOK), f32, V),
            ((8, SEQ, D), bf16, V), ((8, SEQ, D), bf16, V),
        ],
        [(x_own, V)] + [(p, V) for p in attn_pieces] + [(misc, V)],
        flops=10**7, nbytes=6 * 2**20, name="residual_norm",
    )

    def group_exchange(value):
        return lax.all_to_all(value, ("x", "yl"), split_axis=0, concat_axis=0, tiled=True)

    dn, mix, kept = [], [], []
    group_rows = [group_exchange(n2_a), group_exchange(n2_b)]
    for half, rows in enumerate(group_rows):
        if half:
            rows, _ = lax.optimization_barrier((rows, outs[0]))
        rows_sib = send(rows, dc=1)
        outs = call(
            functools.partial(kernel_expert, half),
            [
                ((8, 80, D), bf16, V), ((8, SEQ, D), bf16, V),
                ((512, D), bf16, V), ((512, D), bf16, V), ((512, F), bf16, V), ((512, 1024), bf16, V),
            ]
            + [((2, 80, D), bf16, V)] * 4
            + [((2, SEQ, D), bf16, V)] * 4,
            [(where, S), (misc, V), (rows, A), (rows_sib, A), (e_full, A)] + [(p, A) for p in g_all],
            [
                pltpu.VMEM((16, SEQ, D), bf16), pltpu.VMEM((16, 80, D), bf16),
                pltpu.VMEM((D, 1024), bf16), pltpu.VMEM((F, D), bf16),
                pltpu.VMEM((16, SEQ), f32), pltpu.VMEM((16, SEQ), f32), pltpu.VMEM((16, 1024), f32),
                pltpu.SemaphoreType.DMA((2,)), pltpu.SemaphoreType.DMA((32,)), pltpu.SemaphoreType.DMA((32,)),
            ],
            flops=6 * 10**9, nbytes=30 * 2**20, name="experts",
        )
        recv = [send(v, dc=1) for v in outs[6:10]]
        if half:
            recv, dn[0] = lax.optimization_barrier((recv, dn[0]))
        (summed,) = call(
            kernel_pair_sum, [((8, 80, D), bf16, V)], [(outs[0], V)] + [(v, V) for v in recv],
            flops=10**7, nbytes=6 * 2**20, name="pair_sum",
        )
        dn.append(group_exchange(summed))
        mix.append((outs[1], outs[10:14]))
        kept.extend(outs[2:6])
    kept[0], _ = lax.optimization_barrier((kept[0], summed))
    (e_grad,) = call(
        kernel_expert_grads, [((D, D), bf16, V)], [(v, V) for v in kept],
        flops=6 * 10**9, nbytes=14 * 2**20, name="expert_gradients",
    )
    mix[1], _ = lax.optimization_barrier((mix[1], e_grad))
    mix_sums = [(v, V) for own, sib in mix for v in [own] + [send(piece, dc=1) for piece in sib]]
    mix_sum = call(
        kernel_mix_sum, [((4, TOK, D), bf16, V)] * 2, [(where, S)] + mix_sums,
        flops=10**7, nbytes=10 * 2**20, name="mix_sum",
    )
    dn[1], e_grad, mix_sum = lax.optimization_barrier((dn[1], e_grad, mix_sum))
    e_sum = lax.psum_scatter(e_grad, ("z", "yh"), scatter_dimension=0, tiled=True)
    dresid, dattn, small_grad = call(
        kernel_home,
        [((TOK, D), f32, V), ((TOK, D), bf16, V), ((32, D), f32, V)],
        [(g_own, V), (resid, V), (n2, V), (gates, V), (misc, V), (dn[0], V), (dn[1], V)],
        [pltpu.VMEM((16, TOK), f32)],
        flops=10**8, nbytes=6 * 2**20, name="home_gradient",
    )
    da_z = [dattn] + [send(dattn, dz=j) for j in (1, 2, 3)]
    da_all = da_z + [send(item, dc=1) for item in da_z]
    mix_keep, mix_give = mix_sum
    mix_recv = send(mix_give, dl=1)
    da_all, mix_recv = lax.optimization_barrier((da_all, mix_recv))
    outs = call(
        kernel_back,
        [((4, TOK, D), f32, V), ((4, TOK, D), bf16, V)]
        + [((2, 4, 48, QKVM), bf16, A)] * 4
        + [((48, D), bf16, A)] * 4,
        [
            (where, S), (normed, V), (qk_b, V), (v_b, V), (mixed, V), (small_grad, V), (cos_full, V), (sin_full, V),
        ]
        + [(p, V) for p in x_all + da_all]
        + dense,
        [
            pltpu.VMEM((D, QKVM), bf16), pltpu.VMEM((HQ, D), bf16), pltpu.VMEM((ROWS, D), bf16),
            pltpu.VMEM((ROWS, HQ), bf16), pltpu.VMEM((ROWS, QK), f32), pltpu.VMEM((ROWS, QKVM), bf16),
            pltpu.VMEM((D, QKVM), bf16), pltpu.VMEM((HQ, D), bf16),
            pltpu.SemaphoreType.DMA((32,)), pltpu.SemaphoreType.DMA((4,)), pltpu.SemaphoreType.DMA((36,)),
        ],
        flops=6 * ROWS * D * 512, nbytes=20 * 2**20, name="attention_back",
    )
    dn1_own, dn1_sib = outs[:2]
    wg, og = outs[2:6], outs[6:10]
    wg = [wg[0]] + [send(wg[k], dx=k) for k in (1, 2, 3)]
    og = [og[0]] + [send(og[k], dx=k) for k in (1, 2, 3)]
    dn1_parts = core_sum(dn1_own, dn1_sib)
    wg, og, dn1_parts = lax.optimization_barrier((wg, og, dn1_parts))
    (token_grad,) = call(
        kernel_token_grad, [((TOK, D), bf16, V)],
        [(x_own, V), (dresid, V)] + [(p, V) for p in team_sum(dn1_parts)] + [(misc, V)],
        flops=10**7, nbytes=3 * 2**20, name="token_gradient",
    )
    ge_out = e_sum[:, 1024:].reshape(3, 8, 8, 512).transpose(1, 0, 2, 3).reshape(8, 24, 512)
    ge = jnp.concatenate([e_sum[:, :1024].reshape(8, 24, 1024), ge_out], axis=2)
    ge = lax.all_to_all(ge, ("x", "c"), split_axis=0, concat_axis=0, tiled=True).astype(f32)
    ge_in = ge[:, :, :1024]
    ge_out = ge[:, :, 1024:].reshape(8, 3, 8, 512).transpose(0, 2, 1, 3).reshape(8, 8, D)

    mix_pieces = call(
        kernel_mix_pair, [((TOK, D), bf16, V)] * 4,
        [(where, S), (mix_keep, V), (mix_recv, V)],
        flops=10**6, nbytes=5 * 2**20, name="mix_pair",
    )
    mix_pieces = [mix_pieces[0]] + [send(mix_pieces[k], dx=k) for k in (1, 2, 3)]
    (block_out,) = call(
        kernel_block_out, [((TOK, D), bf16, V)], [(g_own, V), (resid, V)] + [(p, V) for p in mix_pieces],
        flops=10**7, nbytes=5 * 2**20, name="block_output",
    )

    w_keep, w_give, o_keep, o_give = call(
        kernel_dense_sum,
        [((4, 48, QKVM), bf16, V)] * 2 + [((48, D), bf16, V)] * 2,
        [(where, S)] + [(v, V) for v in wg + og],
        flops=10**6, nbytes=5 * 2**20, name="dense_sum",
    )
    heads = (w_keep.astype(f32) + send(w_give, dh=1, dl=1).astype(f32)).astype(bf16).reshape(16, 12, QKVM)
    heads = lax.all_to_all(heads, ("z", "c", "yl"), split_axis=0, concat_axis=0, tiled=True).astype(f32)
    heads = heads.reshape(8, 2, 12, QKVM).sum(axis=1)
    back = (o_keep.astype(f32) + send(o_give, dh=1, dl=1).astype(f32)).astype(bf16).reshape(4, 12, D)
    me = ic * 2 + il
    d_o = pick(back, 0, me).astype(f32) + send(pick(back, 0, me ^ 1), dl=1).astype(f32)
    d_o = d_o + send(pick(back, 0, me ^ 2), dc=1).astype(f32) + send(pick(back, 0, me ^ 3), dc=1, dl=1).astype(f32)
    dq = heads[:, :, :HQ].transpose(1, 0, 2).reshape(12, D)
    dk = heads[:, :, HQ:QK].transpose(1, 0, 2).reshape(12, 512)
    dv = heads[:, :, QK:QKV].transpose(1, 0, 2).reshape(12, 512)
    d_small = heads[:, :, QKV:].sum(axis=0)
    return (
        block_out.reshape(2, SEQ, D),
        token_grad.reshape(2, SEQ, D),
        d_small[:, 16],
        dq,
        dk,
        dv,
        d_o,
        d_small[:, 17],
        d_small[:, :16],
        ge_in,
        ge_out,
    )


def solution(mesh):
    devices = mesh.devices.reshape(DIMS) if hasattr(mesh, "devices") else None
    fine = Mesh(devices, AX)
    every = ("z", "yh", "x", "c", "yl")
    dp = ("z", "yh", "x", "c")
    in_specs = (
        P(every, None, None), P(every, None), P(every, None, None), P(every, None, None), P(every),
        P(every, None), P(every, None), P(every, None), P(every, None), P(every), P(every, None),
        P("yl", dp, None), P("yl", dp, None),
    )
    out_specs = (
        P(every, None, None), P(every, None, None), P(every), P(every, None), P(every, None),
        P(every, None), P(every, None), P(every), P(every, None), P("yl", dp, None), P("yl", dp, None),
    )
    return jax.shard_map(on_device, mesh=fine, in_specs=in_specs, out_specs=out_specs, check_vma=False)
```

time: 749 us -> 482 us (0.64)
  starting transfers between devices: 314 us -> 112 us
  waiting for transfers between devices: 293 us -> 137 us
  blocking collectives: 0 us -> 52.6 us
  Pallas kernels: 99 us -> 129 us
  between operations: 2.5 us -> 15.2 us
    ppermute x128 -> x72, starting transfers between devices: 249 us -> 89 us  [send(): return lax.ppermute(value, AX, pairs)]
    ppermute x128 -> x72, waiting for transfers between devices: 272 us -> 116 us  [send(): return lax.ppermute(value, AX, pairs)]
    all_to_all x0 -> x3, blocking collectives: none -> 52.6 us  [the longest x1 23.3 us: group_exchange(): lax.all_to_all(value, ('x', 'yl'), split_axis=0, concat_axis=0, tiled=True)]
    all_to_all x6 -> x5, starting transfers between devices: 65 us -> 23 us  [the longest x3 14.5 us: group_exchange(): lax.all_to_all(value, ('x', 'yl'), split_axis=0, concat_axis=0, tiled=True)]
    pallas_call x11 -> x16, Pallas kernels: 99 us -> 129 us  [call(): pl.pallas_call(body, out_shape=[jax.ShapeDtypeStruct(shape, dtype) for sh...]
    all_to_all x6 -> x5, waiting for transfers between devices: 21.3 us -> 21.4 us  [the longest x3 10.3 us: group_exchange(): lax.all_to_all(value, ('x', 'yl'), split_axis=0, concat_axis=0, tiled=True)]
  transfers between devices with their start and end apart: 134 -> 79, of which waited for: 43 -> 36; matrix products, arithmetic and copies ran while one was open for 2% -> 3% of each run, Pallas kernels for 8% -> 26%
where the time goes in v2:
time: 482 us; the launch traced here: 475 us
  waiting for transfers between devices  137 us (28%)
  Pallas kernels  129 us (27%)
  starting transfers between devices  112 us (23%)
  blocking collectives  52.6 us (11%)
  local copies, waits for them, and re-layouts  21.5 us (4%)
  between operations  15.2 us (3%)
  other arithmetic  7.1 us (1%)
    pallas_call x16, Pallas kernels, call(): pl.pallas_call(body, out_shape=[jax.ShapeDtypeStruct(shape, dtype) for sh...  129 us
    ppermute x72, waiting for transfers between devices, send(): return lax.ppermute(value, AX, pairs)  116 us
    ppermute x72, starting transfers between devices, send(): return lax.ppermute(value, AX, pairs)  89 us
    all_to_all x1, blocking collectives, group_exchange(): lax.all_to_all(value, ('x', 'yl'), split_axis=0, concat_axis=0, tiled=True)  23.3 us
    all_to_all x1, blocking collectives, on_device(): lax.all_to_all(e_pack, ('x', 'c'), split_axis=0, concat_axis=0, tiled=True)  14.8 us
    all_to_all x3, starting transfers between devices, group_exchange(): lax.all_to_all(value, ('x', 'yl'), split_axis=0, concat_axis=0, tiled=True)  14.5 us
    all_to_all x1, blocking collectives, on_device(): lax.all_to_all(heads, ('z', 'c', 'yl'), split_axis=0, concat_axis=0, tile...  14.4 us
    all_to_all x3, waiting for transfers between devices, group_exchange(): lax.all_to_all(value, ('x', 'yl'), split_axis=0, concat_axis=0, tiled=True)  10.3 us
  transfers between devices with their start and end apart: 79, of which 36 were waited for; matrix products, arithmetic and copies ran while one was open for 3% of the time, Pallas kernels for 26%

profile of v2, /device:TPU:1, one launch (start us, length us, event | category | flops | bytes accessed | tf_op | source)
XLA Modules:
  0.0 474.5 jit_solution(10125887495305237385)
XLA Ops:
  12.4 14.4 %all_to_all.40 = bf16[16,12,384]{2,1,0:T(8,128)(2,1)S(1)} all-to-all(bf16[16,12,384]{2,1,0:T(8,128)(2,1)S(1)} %bitcast.76), channel_id=1, replica_groups=mesh['z'=4,'yh'=2,'x'=4,'c'=2,'yl'=2] {'z','c','yl'}, dimensions={0} | all-to-all | bytes 294912 | tf_op jit(solution)/shard_map/all_to_all | solution.py:593
  27.5 14.8 %all_to_all.41 = bf16[8,24,1536]{2,1,0:T(8,128)(2,1)S(1)} all-to-all(bf16[8,24,1536]{2,1,0:T(8,128)(2,1)S(1)} %pad_maximum_fusion.1), channel_id=1, replica_groups=mesh['z'=4,'yh'=2,'x'=4,'c'=2,'yl'=2] {'x','c'}, dimensions={0} | all-to-all | bytes 1179648 | tf_op jit(solution)/shard_map/all_to_all | solution.py:615
  57.2 7.8 %collective-permute-done.23 = bf16[144,1536]{1,0:T(8,128)(2,1)S(1)} collective-permute-done((bf16[144,1536]{1,0:T(8,128)(2,1)S(1)}, bf16[144,1536]{1,0:T(8,128)(2,1)S(1)}, u32[]{:S(2)}, u32[]{:S(2)}) %collective-permute-start.23) | collective-permute-done | bytes 442400 | tf_op jit(solution)/shard_map/ppermute | solution.py:47
  72.7 7.5 %collective-permute-done.5.rest_2_ = bf16[144,1536]{1,0:T(8,128)(2,1)S(1)} collective-permute-done((bf16[144,1536]{1,0:T(8,128)(2,1)S(1)}, bf16[144,1536]{1,0:T(8,128)(2,1)S(1)}, u32[]{:S(2)}, u32[]{:S(2)}) %collective-permute-start.5) | collective-permute-done | bytes 442400 | tf_op jit(solution)/shard_map/ppermute | solution.py:47
  80.2 5.5 %collective-permute-start.14 = (bf16[48,1536]{1,0:T(8,128)(2,1)}, bf16[48,1536]{1,0:T(8,128)(2,1)}, u32[]{:S(2)}, u32[]{:S(2)}) collective-permute-start(bf16[48,1536]{1,0:T(8,128)(2,1)} %reshape.126), channel_id=1, source_target_pairs={{0,17},{1,16},{2,19},{3,18},{4,21},{5,20},{6,23},{7,22},{8,25},{9,... | collective-permute-start | bytes 442376 | tf_op jit(solution)/shard_map/ppermute | solution.py:47
  98.9 13.0 %collective-permute-done.17.rest_15_.rest_23_ = bf16[48,1536]{1,0:T(8,128)(2,1)S(1)} collective-permute-done((bf16[48,1536]{1,0:T(8,128)(2,1)S(1)}, bf16[48,1536]{1,0:T(8,128)(2,1)S(1)}, u32[]{:S(2)}, u32[]{:S(2)}) %collective-permute-start.17) | collective-permute-done | bytes 147488 | tf_op jit(solution)/shard_map/ppermute | solution.py:47
  120.1 12.1 %attention.1 = (bf16[1024,1536]{1,0:T(8,128)(2,1)}, bf16[1024,256]{1,0:T(8,128)(2,1)}, bf16[1024,128]{1,0:T(8,128)(2,1)}, bf16[1024,192]{1,0:T(8,128)(2,1)}, bf1...) custom-call(s32[5]{0:T(128)} %stack.62.where, f32[256,128]{1,0:T(8,128)} %constant.49.clone.cos_ref, ...), custom_call_target="tpu_custom_call" | custom-call | flops 161061 | bytes 1258 | tf_op jit(solution)/shard_map/attention/pallas_call | solution.py:536
  145.5 9.7 %collective-permute-done.19.p1 = bf16[128,1536]{1,0:T(8,128)(2,1)S(1)} collective-permute-done((bf16[128,1536]{1,0:T(8,128)(2,1)}, bf16[128,1536]{1,0:T(8,128)(2,1)S(1)}, u32[]{:S(2)}, u32[]{:S(2)}) %collective-permute-start.19) | collective-permute-done | bytes 393248 | tf_op jit(solution)/shard_map/ppermute | solution.py:47
  155.2 9.3 %collective-permute-done.20.p2 = bf16[128,1536]{1,0:T(8,128)(2,1)S(1)} collective-permute-done((bf16[128,1536]{1,0:T(8,128)(2,1)}, bf16[128,1536]{1,0:T(8,128)(2,1)S(1)}, u32[]{:S(2)}, u32[]{:S(2)}) %collective-permute-start.20) | collective-permute-done | bytes 393248 | tf_op jit(solution)/shard_map/ppermute | solution.py:47
  169.3 23.3 %all_to_all.42.n2_own = bf16[8,64,1536]{2,1,0:T(8,128)(2,1)S(1)} all-to-all(bf16[8,64,1536]{2,1,0:T(8,128)(2,1)} %get-tuple-element.155), channel_id=1, replica_groups=mesh['z'=4,'yh'=2,'x'=4,'c'=2,'yl'=2] {'x','yl'}, dimensions={0} | all-to-all | bytes 3145728 | tf_op jit(solution)/shard_map/all_to_all | solution.py:657
  198.6 20.3 %experts.2 = (bf16[8,80,1536]{2,1,0:T(8,128)(2,1)}, bf16[8,64,1536]{2,1,0:T(8,128)(2,1)}, bf16[512,1536]{1,0:T(8,128)(2,1)}, bf16[512,1536]{1,0:T(8,128)(2,1)}, ...) custom-call(s32[5]{0:T(128)} %stack.62.where, ...), custom_call_target="tpu_custom_call" | custom-call | flops 600000 | bytes 3145 | tf_op jit(solution)/shard_map/experts/pallas_call | solution.py:536
  228.7 7.1 %all-to-all-start.4 = ((bf16[8,80,1536]{2,1,0:T(8,128)(2,1)}), bf16[8,80,1536]{2,1,0:T(8,128)(2,1)S(1)}, u32[]{:S(2)}, u32[]{:S(2)}) async-start(bf16[8,80,1536]{2,1,0:T(8,128)(2,1)} %pair_sum.2), calls=%async_computation.4 | async-start | bytes 3932160 | tf_op jit(solution)/shard_map/all_to_all | solution.py:657
  235.7 20.4 %experts.3 = (bf16[8,80,1536]{2,1,0:T(8,128)(2,1)}, bf16[8,64,1536]{2,1,0:T(8,128)(2,1)}, bf16[512,1536]{1,0:T(8,128)(2,1)}, bf16[512,1536]{1,0:T(8,128)(2,1)}, ...) custom-call(s32[5]{0:T(128)} %stack.62.where, ...), custom_call_target="tpu_custom_call" | custom-call | flops 600000 | bytes 3145 | tf_op jit(solution)/shard_map/experts/pallas_call | solution.py:536
  275.2 10.9 %expert_gradients.1 = bf16[1536,1536]{1,0:T(8,128)(2,1)} custom-call(bf16[512,1536]{1,0:T(8,128)(2,1)} %get-tuple-element.177.disp_a, bf16[512,1536]{1,0:T(8,128)(2,1)} %get-tuple-element.178.dslot_a, bf16[512,512]{1,0:T(8,128)(2,1)} %get-tuple-element.179.hid_a, bf16[512,1024]{1,0:T(8,128)(2,1)} %get-tuple-element.180.dgu_a, ...), custom_call_target="tpu_custom_call" | custom-call | flops 600000 | bytes 1468 | tf_op jit(solution)/shard_map/expert_gradients/pallas_call | solution.py:536
  290.0 5.1 %mix_sum.1 = (bf16[4,128,1536]{2,1,0:T(8,128)(2,1)}, bf16[4,128,1536]{2,1,0:T(8,128)(2,1)}) custom-call(s32[5]{0:T(128)} %stack.62.where, bf16[8,64,1536]{2,1,0:T(8,128)(2,1)} %get-tuple-element.185.refs_0_, bf16[2,64,1536]{2,1,0:T(8,128)(2,1)} %copy-done.36, bf16[2,64,1536]{2,1,0:T(8,128)(2,1)} %copy-done.37, bf16[2,64,1536]{2,1,0:T(8,128)(2,1)} %copy-done.38, ...), custom_call_target="tpu_custom_call" | custom-call | flops 1000 | bytes 1048 | tf_op jit(solution)/shard_map/mix_sum/pallas_call | solution.py:536
  295.1 5.6 %all-to-all-done.5.dn_b = bf16[8,80,1536]{2,1,0:T(8,128)(2,1)S(1)} async-done(((bf16[8,80,1536]{2,1,0:T(8,128)(2,1)}), bf16[8,80,1536]{2,1,0:T(8,128)(2,1)S(1)}, u32[]{:S(2)}, u32[]{:S(2)}) %all-to-all-start.5) | async-done | bytes 1966112 | tf_op jit(solution)/shard_map/all_to_all | solution.py:657
  313.4 7.3 %collective-permute-done.46.rest_9_ = bf16[128,1536]{1,0:T(8,128)(2,1)S(1)} collective-permute-done((bf16[128,1536]{1,0:T(8,128)(2,1)}, bf16[128,1536]{1,0:T(8,128)(2,1)S(1)}, u32[]{:S(2)}, u32[]{:S(2)}) %collective-permute-start.46) | collective-permute-done | bytes 393248 | tf_op jit(solution)/shard_map/ppermute | solution.py:47
  324.9 8.5 %collective-permute-done.47.rest_10_ = bf16[128,1536]{1,0:T(8,128)(2,1)S(1)} collective-permute-done((bf16[128,1536]{1,0:T(8,128)(2,1)}, bf16[128,1536]{1,0:T(8,128)(2,1)S(1)}, u32[]{:S(2)}, u32[]{:S(2)}) %collective-permute-start.47) | collective-permute-done | bytes 393248 | tf_op jit(solution)/shard_map/ppermute | solution.py:47
  339.7 8.0 %collective-permute-done.53.recv_ref = bf16[4,128,1536]{2,1,0:T(8,128)(2,1)S(1)} collective-permute-done((bf16[4,128,1536]{2,1,0:T(8,128)(2,1)}, bf16[4,128,1536]{2,1,0:T(8,128)(2,1)S(1)}, u32[]{:S(2)}, u32[]{:S(2)}) %collective-permute-start.53) | collective-permute-done | bytes 1572896 | tf_op jit(solution)/shard_map/ppermute | solution.py:47
  347.8 23.8 %attention_back.1 = (f32[4,128,1536]{2,1,0:T(8,128)}, bf16[4,128,1536]{2,1,0:T(8,128)(2,1)}, bf16[2,4,48,384]{3,2,1,0:T(8,128)(2,1)}, bf16[2,4,48,384]{3,2,1,0:T...) custom-call(s32[5]{0:T(128)} %stack.62.where, ...), custom_call_target="tpu_custom_call" | custom-call | flops 483183 | bytes 2097 | tf_op jit(solution)/shard_map/attention_back/pallas_call | solution.py:536
  380.0 7.7 %collective-permute-done.60.refs_5_ = bf16[48,1536]{1,0:T(8,128)(2,1)S(1)} collective-permute-done((bf16[48,1536]{1,0:T(8,128)(2,1)}, bf16[48,1536]{1,0:T(8,128)(2,1)S(1)}, u32[]{:S(2)}, u32[]{:S(2)}) %collective-permute-start.60) | collective-permute-done | bytes 147488 | tf_op jit(solution)/shard_map/ppermute | solution.py:47
  408.6 6.1 %collective-permute-done.55.rest_2_ = bf16[128,1536]{1,0:T(8,128)(2,1)S(1)} collective-permute-done((bf16[128,1536]{1,0:T(8,128)(2,1)}, bf16[128,1536]{1,0:T(8,128)(2,1)S(1)}, u32[]{:S(2)}, u32[]{:S(2)}) %collective-permute-start.55) | collective-permute-done | bytes 393248 | tf_op jit(solution)/shard_map/ppermute | solution.py:47
  414.7 6.9 %collective-permute-done.56.rest_3_ = bf16[128,1536]{1,0:T(8,128)(2,1)S(1)} collective-permute-done((bf16[128,1536]{1,0:T(8,128)(2,1)}, bf16[128,1536]{1,0:T(8,128)(2,1)S(1)}, u32[]{:S(2)}, u32[]{:S(2)}) %collective-permute-start.56) | collective-permute-done | bytes 393248 | tf_op jit(solution)/shard_map/ppermute | solution.py:47
  441.3 8.2 %all-to-all-done.6 = bf16[16,12,384]{2,1,0:T(8,128)(2,1)S(1)} async-done(((bf16[16,12,384]{2,1,0:T(8,128)(2,1)}), bf16[16,12,384]{2,1,0:T(8,128)(2,1)S(1)}, u32[]{:S(2)}, u32[]{:S(2)}) %all-to-all-start.6) | async-done | bytes 147488 | tf_op jit(solution)/shard_map/all_to_all | solution.py:770
  (352 shorter events, 196.0 us)
Async XLA Ops:
  7.2 191.3 %all-gather.2.cloned.1.call-start = ((), (), s32[]{:S(2)}) async-start(), calls=%async_computation.9 | async-start | bytes 5308416 | tf_op jit(solution)/shard_map/all_gather | solution.py:618
  47.7 21.7 %collective-permute-start.24 = (bf16[144,1536]{1,0:T(8,128)(2,1)S(1)}, bf16[144,1536]{1,0:T(8,128)(2,1)}, u32[]{:S(2)}, u32[]{:S(2)}) collective-permute-start(bf16[144,1536]{1,0:T(8,128)(2,1)S(1)} %get-tuple-element.262.gx_ref), channel_id=1, source_target_pairs={{0,12},{1,13},{2,14},{3,15},{4,8},{5,9},{6,10},{7,11},{8,4},{9,5},... | collective-permute-start | bytes 1327112 | tf_op jit(solution)/shard_map/ppermute | solution.py:47
  50.2 22.5 %collective-permute-start.4 = (bf16[144,1536]{1,0:T(8,128)(2,1)S(1)}, bf16[144,1536]{1,0:T(8,128)(2,1)S(1)}, u32[]{:S(2)}, u32[]{:S(2)}) collective-permute-start(bf16[144,1536]{1,0:T(8,128)(2,1)S(1)} %get-tuple-element.136.rest_0_.xo), channel_id=1, source_target_pairs={{0,32},{1,33},{2,34},{3,35},{4,36},{5,37},{6,38},{7,39},{8,40},{9,... | collective-permute-start | bytes 1327112 | tf_op jit(solution)/shard_map/ppermute | solution.py:47
  52.7 27.5 %collective-permute-start.5 = (bf16[144,1536]{1,0:T(8,128)(2,1)S(1)}, bf16[144,1536]{1,0:T(8,128)(2,1)S(1)}, u32[]{:S(2)}, u32[]{:S(2)}) collective-permute-start(bf16[144,1536]{1,0:T(8,128)(2,1)S(1)} %get-tuple-element.136.rest_0_.xo), channel_id=1, source_target_pairs={{0,64},{1,65},{2,66},{3,67},{4,68},{5,69},{6,70},{7,71},{8,72},{9,... | collective-permute-start | bytes 1327112 | tf_op jit(solution)/shard_map/ppermute | solution.py:47
  55.0 25.2 %collective-permute-start.6 = (bf16[144,1536]{1,0:T(8,128)(2,1)S(1)}, bf16[144,1536]{1,0:T(8,128)(2,1)}, u32[]{:S(2)}, u32[]{:S(2)}) collective-permute-start(bf16[144,1536]{1,0:T(8,128)(2,1)S(1)} %get-tuple-element.136.rest_0_.xo), channel_id=1, source_target_pairs={{0,96},{1,97},{2,98},{3,99},{4,100},{5,101},{6,102},{7,103},{8,104... | collective-permute-start | bytes 1327112 | tf_op jit(solution)/shard_map/ppermute | solution.py:47
  70.9 61.9 %collective-permute-start.25 = (bf16[4,144,1536]{2,1,0:T(8,128)(2,1)S(1)}, bf16[4,144,1536]{2,1,0:T(8,128)(2,1)}, u32[]{:S(2)}, u32[]{:S(2)}) collective-permute-start(bf16[4,144,1536]{2,1,0:T(8,128)(2,1)S(1)} %pad_maximum_fusion.rest_0_), channel_id=1, source_target_pairs={{0,1},{1,0},{2,3},{3,2},{4,5},{5,4},{6,7},{7,6},{8,9},{9,8},{10,11... | collective-permute-start | bytes 5308424 | tf_op jit(solution)/shard_map/ppermute | solution.py:47
  93.4 22.9 %collective-permute-start.11 = (bf16[2,4,48,384]{3,2,1,0:T(8,128)(2,1)S(1)}, bf16[2,4,48,384]{3,2,1,0:T(8,128)(2,1)S(1)}, u32[]{:S(2)}, u32[]{:S(2)}) collective-permute-start(bf16[2,4,48,384]{3,2,1,0:T(8,128)(2,1)S(1)} %pad_maximum_fusion.4.rest_8_.rest_16_), channel_id=1, source_target_pairs={{0,4},{1,5},{2,6},{3,7},{4,0},{5,1},{6,2},{7,3},{8,12},{9,13},{10,... | collective-permute-start | bytes 884744 | tf_op jit(solution)/shard_map/ppermute | solution.py:47
  93.4 23.0 %collective-permute-start.12 = (bf16[2,4,48,384]{3,2,1,0:T(8,128)(2,1)S(1)}, bf16[2,4,48,384]{3,2,1,0:T(8,128)(2,1)S(1)}, u32[]{:S(2)}, u32[]{:S(2)}) collective-permute-start(bf16[2,4,48,384]{3,2,1,0:T(8,128)(2,1)S(1)} %pad_maximum_fusion.4.rest_8_.rest_16_), channel_id=1, source_target_pairs={{0,8},{1,9},{2,10},{3,11},{4,12},{5,13},{6,14},{7,15},{8,0},{9,1},... | collective-permute-start | bytes 884744 | tf_op jit(solution)/shard_map/ppermute | solution.py:47
  94.6 22.3 %collective-permute-start.13 = (bf16[2,4,48,384]{3,2,1,0:T(8,128)(2,1)S(1)}, bf16[2,4,48,384]{3,2,1,0:T(8,128)(2,1)S(1)}, u32[]{:S(2)}, u32[]{:S(2)}) collective-permute-start(bf16[2,4,48,384]{3,2,1,0:T(8,128)(2,1)S(1)} %pad_maximum_fusion.4.rest_8_.rest_16_), channel_id=1, source_target_pairs={{0,12},{1,13},{2,14},{3,15},{4,8},{5,9},{6,10},{7,11},{8,4},{9,5},... | collective-permute-start | bytes 884744 | tf_op jit(solution)/shard_map/ppermute | solution.py:47
  132.8 31.8 %collective-permute-start.27 = (bf16[4,144,1536]{2,1,0:T(8,128)(2,1)}, bf16[4,144,1536]{2,1,0:T(8,128)(2,1)}, u32[]{:S(2)}, u32[]{:S(2)}) collective-permute-start(bf16[4,144,1536]{2,1,0:T(8,128)(2,1)} %collective-permute-done.25.rest_1_), channel_id=1, source_target_pairs={{0,2},{1,3},{2,0},{3,1},{4,6},{5,7},{6,4},{7,5},{8,10},{9,11},{10,... | collective-permute-start | bytes 5308424 | tf_op jit(solution)/shard_map/ppermute | solution.py:47
  141.8 22.7 %collective-permute-start.20 = (bf16[128,1536]{1,0:T(8,128)(2,1)}, bf16[128,1536]{1,0:T(8,128)(2,1)S(1)}, u32[]{:S(2)}, u32[]{:S(2)}) collective-permute-start(bf16[128,1536]{1,0:T(8,128)(2,1)} %get-tuple-element.146), channel_id=1, source_target_pairs={{0,64},{1,65},{2,66},{3,67},{4,68},{5,69},{6,70},{7,71},{8,72},{9,... | collective-permute-start | bytes 1179656 | tf_op jit(solution)/shard_map/ppermute | solution.py:47
  142.4 22.1 %collective-permute-start.21 = (bf16[128,1536]{1,0:T(8,128)(2,1)}, bf16[128,1536]{1,0:T(8,128)(2,1)S(1)}, u32[]{:S(2)}, u32[]{:S(2)}) collective-permute-start(bf16[128,1536]{1,0:T(8,128)(2,1)} %get-tuple-element.147), channel_id=1, source_target_pairs={{0,96},{1,97},{2,98},{3,99},{4,100},{5,101},{6,102},{7,103},{8,104... | collective-permute-start | bytes 1179656 | tf_op jit(solution)/shard_map/ppermute | solution.py:47
  194.7 26.6 %all-to-all-start.1 = ((bf16[8,64,1536]{2,1,0:T(8,128)(2,1)}), bf16[8,64,1536]{2,1,0:T(8,128)(2,1)S(1)}, u32[]{:S(2)}, u32[]{:S(2)}) async-start(bf16[8,64,1536]{2,1,0:T(8,128)(2,1)} %get-tuple-element.154), calls=%async_computation.1 | async-start | bytes 3145728 | tf_op jit(solution)/shard_map/all_to_all | solution.py:657
  228.7 36.0 %all-to-all-start.4 = ((bf16[8,80,1536]{2,1,0:T(8,128)(2,1)}), bf16[8,80,1536]{2,1,0:T(8,128)(2,1)S(1)}, u32[]{:S(2)}, u32[]{:S(2)}) async-start(bf16[8,80,1536]{2,1,0:T(8,128)(2,1)} %pair_sum.2), calls=%async_computation.4 | async-start | bytes 3932160 | tf_op jit(solution)/shard_map/all_to_all | solution.py:657
  269.3 31.5 %all-to-all-start.5 = ((bf16[8,80,1536]{2,1,0:T(8,128)(2,1)}), bf16[8,80,1536]{2,1,0:T(8,128)(2,1)S(1)}, u32[]{:S(2)}, u32[]{:S(2)}) async-start(bf16[8,80,1536]{2,1,0:T(8,128)(2,1)} %pair_sum.3), calls=%async_computation.5 | async-start | bytes 3932160 | tf_op jit(solution)/shard_map/all_to_all | solution.py:657
  272.9 176.6 %reduce-scatter.2.cloned.1.call-start = ((), (), s32[]{:S(2)}) async-start(), calls=%async_computation.10 | async-start | bytes 5308416 | tf_op jit(solution)/shard_map/reduce_scatter | solution.py:704
  302.1 45.7 %collective-permute-start.53 = (bf16[4,128,1536]{2,1,0:T(8,128)(2,1)}, bf16[4,128,1536]{2,1,0:T(8,128)(2,1)S(1)}, u32[]{:S(2)}, u32[]{:S(2)}) collective-permute-start(bf16[4,128,1536]{2,1,0:T(8,128)(2,1)} %get-tuple-element.208), channel_id=1, source_target_pairs={{0,1},{1,0},{2,3},{3,2},{4,5},{5,4},{6,7},{7,6},{8,9},{9,8},{10,11... | collective-permute-start | bytes 4718600 | tf_op jit(solution)/shard_map/ppermute | solution.py:47
  307.1 26.2 %collective-permute-start.47 = (bf16[128,1536]{1,0:T(8,128)(2,1)}, bf16[128,1536]{1,0:T(8,128)(2,1)S(1)}, u32[]{:S(2)}, u32[]{:S(2)}) collective-permute-start(bf16[128,1536]{1,0:T(8,128)(2,1)} %get-tuple-element.220.rest_8_), channel_id=1, source_target_pairs={{0,64},{1,65},{2,66},{3,67},{4,68},{5,69},{6,70},{7,71},{8,72},{9,... | collective-permute-start | bytes 1179656 | tf_op jit(solution)/shard_map/ppermute | solution.py:47
  309.6 28.2 %collective-permute-start.48 = (bf16[128,1536]{1,0:T(8,128)(2,1)}, bf16[128,1536]{1,0:T(8,128)(2,1)S(1)}, u32[]{:S(2)}, u32[]{:S(2)}) collective-permute-start(bf16[128,1536]{1,0:T(8,128)(2,1)} %get-tuple-element.220.rest_8_), channel_id=1, source_target_pairs={{0,96},{1,97},{2,98},{3,99},{4,100},{5,101},{6,102},{7,103},{8,104... | collective-permute-start | bytes 1179656 | tf_op jit(solution)/shard_map/ppermute | solution.py:47
  310.7 27.4 %collective-permute-start.49 = (bf16[128,1536]{1,0:T(8,128)(2,1)}, bf16[128,1536]{1,0:T(8,128)(2,1)S(1)}, u32[]{:S(2)}, u32[]{:S(2)}) collective-permute-start(bf16[128,1536]{1,0:T(8,128)(2,1)} %get-tuple-element.220.rest_8_), channel_id=1, source_target_pairs={{0,2},{1,3},{2,0},{3,1},{4,6},{5,7},{6,4},{7,5},{8,10},{9,11},{10,... | collective-permute-start | bytes 1179656 | tf_op jit(solution)/shard_map/ppermute | solution.py:47
  371.6 26.5 %collective-permute-start.63 = (bf16[4,128,1536]{2,1,0:T(8,128)(2,1)}, bf16[4,128,1536]{2,1,0:T(8,128)(2,1)S(1)}, u32[]{:S(2)}, u32[]{:S(2)}) collective-permute-start(bf16[4,128,1536]{2,1,0:T(8,128)(2,1)} %get-tuple-element.237), channel_id=1, source_target_pairs={{0,2},{1,3},{2,0},{3,1},{4,6},{5,7},{6,4},{7,5},{8,10},{9,11},{10,... | collective-permute-start | bytes 4718600 | tf_op jit(solution)/shard_map/ppermute | solution.py:47
  398.1 23.5 %collective-permute-start.56 = (bf16[128,1536]{1,0:T(8,128)(2,1)}, bf16[128,1536]{1,0:T(8,128)(2,1)S(1)}, u32[]{:S(2)}, u32[]{:S(2)}) collective-permute-start(bf16[128,1536]{1,0:T(8,128)(2,1)} %get-tuple-element.213), channel_id=1, source_target_pairs={{0,12},{1,13},{2,14},{3,15},{4,8},{5,9},{6,10},{7,11},{8,4},{9,5},... | collective-permute-start | bytes 1179656 | tf_op jit(solution)/shard_map/ppermute | solution.py:47
  425.9 32.4 %collective-permute-start.64 = (bf16[128,1536]{1,0:T(8,128)(2,1)S(1)}, bf16[128,1536]{1,0:T(8,128)(2,1)S(1)}, u32[]{:S(2)}, u32[]{:S(2)}) collective-permute-start(bf16[128,1536]{1,0:T(8,128)(2,1)S(1)} %copy-done.66), channel_id=1, source_target_pairs={{0,32},{1,33},{2,34},{3,35},{4,36},{5,37},{6,38},{7,39},{8,40},{9,... | collective-permute-start | bytes 1179656 | tf_op jit(solution)/shard_map/ppermute | solution.py:47
  425.9 32.4 %collective-permute-start.65 = (bf16[128,1536]{1,0:T(8,128)(2,1)S(1)}, bf16[128,1536]{1,0:T(8,128)(2,1)S(1)}, u32[]{:S(2)}, u32[]{:S(2)}) collective-permute-start(bf16[128,1536]{1,0:T(8,128)(2,1)S(1)} %copy-done.65), channel_id=1, source_target_pairs={{0,64},{1,65},{2,66},{3,67},{4,68},{5,69},{6,70},{7,71},{8,72},{9,... | collective-permute-start | bytes 1179656 | tf_op jit(solution)/shard_map/ppermute | solution.py:47
  (125 other events, 1203.0 us)
Sparse Core Ops, SparseCore 0:
  43.5 105.4 all-gather.1
  300.9 103.4 reduce-scatter.1
